TPU v7x, 32 devices: a whole 2x2x4 slice. The times are simulated.
32 devices in a mesh: row: 8 (over z, y), col: 4 (over x, core).
Axes of the slice: x: 2, y: 2, z: 4, core: 2. Of those that a mesh axis runs over, the one named last changes fastest.
Arguments:
- feature_map: bfloat16 [512, 32, 2048], P('row', 'col'), may hold values from -6 to 6
- image_ids: int32 [512, 32], P('row', 'col'), may hold values from 0 to 16
- point_weight: bfloat16 [2048, 256], replicated, may hold values from -0.125 to 0.125
- atrous_weight: bfloat16 [3, 3, 3, 2048, 256], replicated, may hold values from -0.046875 to 0.046875
- pool_weight: bfloat16 [2048, 256], replicated, may hold values from -0.125 to 0.125
- project_weight: bfloat16 [1280, 256], replicated, may hold values from -0.15625 to 0.15625
- bn_gain: float32 [6, 256], replicated, may hold values from 0.5 to 1.5
- bn_shift: float32 [6, 256], replicated, may hold values from -2.5 to 2.5
- out_grad: bfloat16 [512, 32, 256], P('row', 'col'), may hold values from -6 to 6
Outputs:
- output: bfloat16 [512, 32, 256], P('row', 'col')
- input_grad: bfloat16 [512, 32, 2048], P('row', 'col')
- point_grad: float32 [2048, 256], P('row')
- atrous_grad: float32 [3, 3, 3, 2048, 256], P(None, None, None, 'row')
- pool_grad: float32 [2048, 256], P('row')
- project_grad: float32 [1280, 256], replicated
- gain_grad: float32 [6, 256], replicated
- shift_grad: float32 [6, 256], replicated
All inputs are finite; a program needn't handle non-finite values.
Results may differ from a plain program's by a relative error of at most 0.012.
Values may be sent and summed in bfloat16 or wider, within the bound.
No kernel may reach another device: no remote copies, remote signals or barrier semaphores. Data moves between devices by JAX's collectives and lax.ppermute only.
A program may use at most 448 MiB of HBM per device.

v0:
```python
from functools import partial

import jax
import jax.numpy as jnp
from jax import lax
from jax.experimental import pallas as pl
from jax.experimental.pallas import tpu as pltpu
from jax.sharding import Mesh, PartitionSpec as P

REACH = 18
IMG_ROWS = 32
EPSILON = 1e-05
PAD = 32
RIM = 24
SWAP = [(0, 1), (1, 0)]
BF = jnp.bfloat16
F32 = jnp.float32
VMEM_LIMIT = 60 * 2**20


def dot(a, b):
    return jnp.dot(a, b, preferred_element_type=F32)


def exact(a, b):
    return jnp.dot(a, b, precision=lax.Precision.HIGHEST, preferred_element_type=F32)


def gate(x, *deps):
    return lax.optimization_barrier((x, deps))[0]


def swap(x, axis):
    return lax.ppermute(x, axis, SWAP)


def z_swap(x, step):
    count = lax.axis_size("z")
    return lax.ppermute(x, "z", [(i, i ^ step) for i in range(count)])


def crossed(x):
    return lax.ppermute(x, ("y", "x"), [(i, 3 - i) for i in range(4)])


def quad(x, axes):
    near, far, last = (
        lax.ppermute(x, axes, [(i, i ^ step) for i in range(4)]) for step in (1, 2, 3)
    )
    return (x + near) + (far + last)


def z_sum(x):
    count = lax.axis_size("z")
    if count == 4:
        return quad(x, "z")
    step = 1
    while step < count:
        x = x + lax.ppermute(x, "z", [(i, i ^ step) for i in range(count)])
        step *= 2
    return x


def plane_sum(x):
    return quad(x, ("y", "x"))


def allsum(x):
    x = plane_sum(z_sum(x))
    return x + swap(x, "k")


def smooth(value):
    return jax.nn.gelu(value, approximate=True)


def smooth_slope(value):
    root = 0.7978845608028654
    square = value * value
    tanh = jnp.tanh(root * (value + 0.044715 * value * square))
    return 0.5 * (1.0 + tanh) + 0.5 * value * (1.0 - tanh * tanh) * root * (
        1.0 + 3 * 0.044715 * square
    )


def moments(value):
    return jnp.stack([jnp.sum(value, axis=0), jnp.sum(value * value, axis=0)])


def place_of(info, n):
    dk, dy, dx = n // 4, n // 2 % 2, n % 2
    col = ((info[1] ^ dx) * 2 + (info[2] ^ dk)) * 8
    return REACH + col, info[0] ^ dy


def tile_copies(info, tiles, window, sems, main=0, rim=0):
    copies = []
    for n, tile in enumerate(tiles):
        col, y = place_of(info, n)
        row = pl.multiple_of(PAD + y * 64, 16)
        copies.append(
            pltpu.make_async_copy(
                tile.at[:, pl.ds(main, 64)],
                window.at[pl.ds(col, 8), pl.ds(row, 64)],
                sems.at[n],
            )
        )
        if rim:
            row = pl.multiple_of(jnp.where(y == 0, PAD + 128, PAD - rim), 16)
            copies.append(
                pltpu.make_async_copy(
                    tile.at[:, pl.ds(main + 64, rim)],
                    window.at[pl.ds(col, 8), pl.ds(row, rim)],
                    sems.at[8 + n],
                )
            )
    for copy in copies:
        copy.start()
    return copies


def place_rims(info, rims, window):
    for dk, rim in enumerate(rims):
        for n in range(4):
            col = REACH + ((n % 2) * 2 + (info[2] ^ dk)) * 8
            row = PAD + 128 if n < 2 else PAD - REACH
            for q in range(8):
                window[col + q, row : row + REACH, :] = rim[n, q, :REACH]


def shift_rows(window, masks, b, q, i, spread, sign, cut, ok=None):
    start = PAD + sign * (i - 1) * spread
    value = window[REACH + q, start : start + 128, :]
    if i != 1:
        keep = masks[b, 1 if sign * (i - 1) > 0 else 0]
        keep = jnp.where(q >= cut, keep, jnp.ones_like(keep))
        if ok is not None:
            keep = jnp.where(ok, keep, jnp.zeros_like(keep))
        value = value * jnp.concatenate([keep] * (value.shape[1] // 128), axis=1)
    elif ok is not None:
        value = jnp.where(ok, value, jnp.zeros_like(value))
    return value


def tap_rows(window, masks, b, col, width, spread, sign, cut):
    return jnp.concatenate(
        [
            jnp.concatenate(
                [shift_rows(window, masks, b, col + u, i, spread, sign, cut) for i in range(3)],
                axis=1,
            )
            for u in range(width)
        ],
        axis=0,
    )


def branch_sum(window, masks, b, col, spread, sign, cut, product, acc, fresh):
    width = 2

    def inside(j, e):
        source = col + e + sign * (j - 1) * spread
        return (source >= 0) & (source < 32) & ((source < cut) == (col + e < cut))

    def center(e):
        return product(1, tap_rows(window, masks, b, col + e, width, spread, sign, cut))

    def side(j, e):
        source = col + e + sign * (j - 1) * spread
        part = product(j, tap_rows(window, masks, b, source, width, spread, sign, cut))
        return jnp.concatenate(
            [
                jnp.where(inside(j, e + u), part[u * 128 : u * 128 + 128], 0.0)
                for u in range(width)
            ],
            axis=0,
        )

    def put(e, value, first):
        value = value.reshape(width, 128, acc.shape[-1])
        if first:
            acc[pl.ds(e, width)] = value
        else:
            acc[pl.ds(e, width)] += value

    dense = spread == REACH // 3
    for e in range(0, 8, width):
        value = center(e)
        if dense:
            value = value + side(0, e) + side(2, e)
        put(e, value, fresh)
    if dense:
        return

    def block(t, carry):
        j, half = (t // 2) * 2, (t % 2) * 4
        some = inside(j, half)
        for e in range(1, 4):
            some = some | inside(j, half + e)

        @pl.when(some)
        def _():
            for e in range(0, 4, width):
                put(half + e, side(j, half + e), False)

        return carry

    lax.fori_loop(0, 4, block, 0)


def forward_kernel(units, spreads, lanes, info, *refs):
    mains, rims = refs[:8], refs[8:10]
    masks, point, weights = refs[10:13]
    outs = refs[13:17]
    window, point_buf, weight_buf, acc, sems, weight_sems = refs[17:]
    iy, ix, ik, cut = info[0], info[1], info[2], info[3]
    copies = tile_copies(info, mains, window, sems)
    loads = []
    for n, b in enumerate(units):
        if b is None:
            loads.append(
                [pltpu.make_async_copy(point.at[:, iy, ix], point_buf, weight_sems.at[n, 0])]
            )
        else:
            loads.append(
                [
                    pltpu.make_async_copy(
                        weights.at[b, i, j, :, iy, ix],
                        weight_buf.at[n, j, i],
                        weight_sems.at[n, 3 * j + i],
                    )
                    for j in range(3)
                    for i in range(3)
                ]
            )
        for copy in loads[n]:
            copy.start()
    place_rims(info, rims, window)
    for copy in copies:
        copy.wait()
    for n, b in enumerate(units):
        for copy in loads[n]:
            copy.wait()
        keep, send = outs[2 * n : 2 * n + 2]
        for dx in (1, 0):
            col = (ix ^ dx) * 16 + ik * 8
            if b is None:
                source = window[pl.ds(REACH + col, 8), PAD : PAD + 128, :].reshape(1024, lanes)
                acc[...] = dot(source, point_buf[...].reshape(lanes, 256)).reshape(8, 128, 256)
            else:

                def product(j, rows, n=n):
                    return dot(rows, weight_buf[n, j].reshape(3 * lanes, 256))

                branch_sum(window, masks, b, col, spreads[b], 1, cut, product, acc, True)
            for dy in range(2):
                row = pl.multiple_of((iy ^ dy) * 64, 64)
                value = acc[:, pl.ds(row, 64), :]
                if (dy if n else dx) == 0:
                    keep[dx if n else dy] = value
                else:
                    send[dx if n else dy] = value.astype(BF)


def input_kernel(chosen, spreads, lanes, pointed, info, *refs):
    count = 8 * (1 + max(c[1] for c in chosen))
    tiles, masks, point, weights = refs[:count], refs[count], refs[count + 1], refs[count + 2]
    rest = refs[count + 3 :]
    if pointed:
        before, edge, strip = rest[:3]
        outs = rest[3:7]
        windows, weight_buf, point_buf, acc, sems, weight_sems = rest[7:]
    else:
        (result,) = rest[:1]
        windows, weight_buf, sems, weight_sems = rest[1:]
        acc = result
    iy, ix, ik, cut = info[0], info[1], info[2], info[3]
    mine = acc.shape[-1]
    fetches, loads = [], []
    for n, (b, first, main, rim) in enumerate(chosen):
        group = tiles[8 * first : 8 * first + 8]
        fetches.append(tile_copies(info, group, windows.at[n], sems.at[n], main, rim))
        if b is None:
            loads.append(
                [pltpu.make_async_copy(point.at[:, iy, ix], point_buf, weight_sems.at[n, 0])]
            )
        else:
            loads.append(
                [
                    pltpu.make_async_copy(
                        weights.at[b, i, j, :, iy, ix],
                        weight_buf.at[n, j, :, :, pl.ds(i * lanes, lanes)],
                        weight_sems.at[n, 3 * j + i],
                    )
                    for j in range(3)
                    for i in range(3)
                ]
            )
        for copy in loads[n]:
            copy.start()

    def times(a, w):
        return lax.dot_general(
            a, w.reshape(mine, w.shape[-1]), (((1,), (1,)), ((), ())), preferred_element_type=F32
        )

    for n, (b, _, _, _) in enumerate(chosen):
        for copy in fetches[n] + loads[n]:
            copy.wait()
        window = windows.at[n]
        for dx in range(2):
            col = (ix ^ dx) * 16 + ik * 8
            if b is None:
                for e in range(0, 8, 2):
                    source = window[pl.ds(REACH + col + e, 2), PAD : PAD + 128, :]
                    value = times(source.reshape(256, lanes), point_buf[...])
                    for u in range(2):
                        pool = jnp.where(col + e + u < cut, edge[...], strip[...])
                        acc[dx, e + u] += (
                            before[dx, e + u] + value[u * 128 : u * 128 + 128] + pool
                        )
            else:

                def product(j, rows, n=n):
                    return times(rows, weight_buf[n, j])

                branch_sum(
                    window, masks, b, col, spreads[b], -1, cut, product, acc.at[dx], n == 0
                )
    if pointed:
        for dx in range(2):
            for dy in range(2):
                row = pl.multiple_of((iy ^ dy) * 64, 64)
                outs[dy * 2 + dx][...] = acc[dx, :, pl.ds(row, 64), :].astype(BF)


def weight_kernel(spread, b, sources, lanes, info, *refs):
    tiles = refs[:8]
    masks, across = refs[8:10]
    pooled = len(sources) > 1
    outs = refs[10 + pooled : -4]
    windows, out, sems, out_sems = refs[-4:]
    cut = info[3]
    parts = out.shape[0]
    each = out.shape[2]
    paired = len(outs) == 2
    fetches = [
        tile_copies(info, tiles, windows.at[n], sems.at[n], main, rim)
        for n, (main, rim) in enumerate(sources)
    ]

    def emit(t, value):
        for z in range(parts):
            out[info[4] ^ z if paired else z, t] = value[z * each : (z + 1) * each].astype(BF)

    for copy in fetches[0]:
        copy.wait()
    window = windows.at[0]
    for j in (1, 0, 2):
        move = (j - 1) * spread
        columns = [p for p in range(32) if 0 <= p + move < 32]
        total = None
        for at in range(0, len(columns), 8):
            group = columns[at : at + 8]
            right = []
            for p in group:
                ok = None if j == 1 else ((p < cut) == (p + move < cut))
                right.append(
                    jnp.concatenate(
                        [shift_rows(window, masks, b, p, i, spread, -1, cut, ok) for i in range(3)],
                        axis=1,
                    )
                )
            first, last = (group[0] + move) * 128, (group[-1] + move + 1) * 128
            part = dot(across[:, first:last], jnp.concatenate(right, axis=0))
            total = part if total is None else total + part
        for i in range(3):
            emit(3 * i + j, total[:, i * lanes : (i + 1) * lanes])
    if len(sources) > 1:
        for copy in fetches[1]:
            copy.wait()
        plain = windows[1, REACH : REACH + 32, PAD : PAD + 128, :].reshape(32 * 128, lanes)
        emit(9, dot(across[...], plain))
        emit(10, refs[10][...])
    if paired:
        moves = [(0, outs[0].at[0]), (3, outs[0].at[1]), (1, outs[1].at[0]), (2, outs[1].at[1])]
        moves = [(out.at[m], target) for m, target in moves]
    else:
        moves = [(out, outs[0])]
    copies = [
        pltpu.make_async_copy(source, target, out_sems.at[n])
        for n, (source, target) in enumerate(moves)
    ]
    for copy in copies:
        copy.start()
    for copy in copies:
        copy.wait()


def collect_kernel(first, count, extras, info, *refs):
    pieces = refs[:4]
    outs = refs[len(refs) - 3 - len(extras) : len(refs) - 2]
    buf, sem = refs[len(refs) - 2 :]
    ix, ik = info[1], info[2]
    if len(extras) == 1:
        outs[1][4] = refs[4][...]
    for n, piece in enumerate(pieces):
        index = (ix ^ (n // 2)) * 2 + (ik ^ (n % 2))
        for t in range(count):
            buf[t, index] = piece[t].astype(F32)
        at = count
        for e, length in enumerate(extras):
            for t in range(length):
                outs[1 + e][index, t] = piece[at + t].astype(F32)
            at += length
    copy = pltpu.make_async_copy(buf, outs[0].at[pl.ds(first, count)], sem)
    copy.start()
    copy.wait()


def pack_kernel(share, info, full, marks, *refs):
    iy, ix = info[0], info[1]
    rims = refs[4]
    for n in range(4):
        other = (iy ^ (n // 2)) * 2 + (ix ^ (n % 2))
        for z in range(full.shape[-1] // (4 * share)):
            lane = pl.multiple_of((z * 4 + other) * share, 128)
            value = jnp.swapaxes(full[:, :, pl.ds(lane, share)], 0, 1)
            refs[n][:, :, z * share : (z + 1) * share] = value

            @pl.when(iy == 0)
            def _(value=value, other=other, z=z):
                rims[other, :, :RIM, z * share : (z + 1) * share] = value[:, :RIM]

            @pl.when(iy == 1)
            def _(value=value, other=other, z=z):
                rims[other, :, :REACH, z * share : (z + 1) * share] = value[:, 64 - REACH :]

    for n in range(4):
        for q in range(8):
            rims[n, q, REACH : REACH + 1, :] = marks[...]


def unpack_kernel(share, info, *refs):
    iy, ix = info[0], info[1]
    full = refs[4]
    for n in range(4):
        other = (iy ^ (n // 2)) * 2 + (ix ^ (n % 2))
        for z in range(full.shape[-1] // (4 * share)):
            lane = pl.multiple_of((z * 4 + other) * share, 128)
            value = refs[n][:, :, z * share : (z + 1) * share]
            full[:, :, pl.ds(lane, share)] = jnp.swapaxes(value, 0, 1)


def across_kernel(share, info, *refs):
    tiles, out, rows, zero = refs[:8], *refs[8:11]
    window, acc, sems = refs[11:]
    ik, cut = info[2], info[3]
    for copy in tile_copies(info, tiles, window, sems):
        copy.wait()
    acc[...] = jnp.zeros_like(acc)
    for q in range(32):
        value = window[REACH + q, PAD : PAD + 128, :]
        turned = value.T
        for z in range(turned.shape[0] // share):
            low = turned[z * share : z * share + share // 2]
            high = turned[z * share + share // 2 : (z + 1) * share]
            out[z * share // 2 : (z + 1) * share // 2, q * 128 : (q + 1) * 128] = jnp.where(
                ik == 0, low, high
            )
        acc[(q >= cut).astype(jnp.int32)] += value.astype(F32)
    rows[...] = acc[1]
    zero[...] = jnp.sum(acc[0], axis=0, keepdims=True)


VMEM = pl.BlockSpec(memory_space=pltpu.VMEM)
SMEM = pl.BlockSpec(memory_space=pltpu.SMEM)
ANY = pl.BlockSpec(memory_space=pl.ANY)


def call(kernel, name, flops, in_specs, out_shape, scratch, args, out_specs=None, aliases=None):
    return pl.pallas_call(
        kernel,
        name=name,
        in_specs=in_specs,
        out_specs=out_specs or jax.tree.map(lambda _: VMEM, out_shape),
        out_shape=out_shape,
        input_output_aliases=aliases or {},
        scratch_shapes=scratch,
        compiler_params=pltpu.CompilerParams(vmem_limit_bytes=VMEM_LIMIT),
        cost_estimate=pl.CostEstimate(flops=flops, bytes_accessed=10**7, transcendentals=0),
    )(*args)


def per_device(
    feature_map,
    image_ids,
    point_weight,
    atrous_weight,
    pool_weight,
    project_weight,
    bn_gain,
    bn_shift,
    out_grad,
):
    rows, cols, chans = feature_map.shape
    feat = point_weight.shape[1]
    pixels = rows * cols
    zs = lax.axis_size("z")
    axes = ("k", "x", "y", "z")
    iz, iy, ix, ik = (lax.axis_index(a) for a in ("z", "y", "x", "k"))
    row_count = 2 * zs
    total = float(pixels * row_count * 4)
    images = rows * row_count // IMG_ROWS + 1
    share = chans // (4 * zs)
    mine = chans // 4
    spreads = [REACH * (b + 1) // 3 for b in range(3)]
    def pick(first, second, index):
        return jnp.where(index == 0, first, second)

    def rim(x, depth):
        return pick(x[:, :depth], x[:, rows - depth :], iy)

    def beyond(x, dy, dx):
        pairs = []
        for z in range(zs):
            for y in range(2):
                far = z - 1 + 2 * y
                if 0 <= far < zs:
                    for i in range(2):
                        target = (far * 2 + (y ^ dy)) * 2 + (i ^ dx)
                        pairs.append(((z * 2 + y) * 2 + i, target))
        return lax.ppermute(x, ("z", "y", "x"), pairs)

    with jax.named_scope("marks"):
        strip_own = jnp.max(image_ids, axis=1)
        edge_own = pick(strip_own[:REACH], strip_own[rows - REACH :], iy)
        zero_own = jnp.sum((image_ids[0] == 0).astype(jnp.int32))
        marks = jnp.concatenate([strip_own, edge_own, zero_own[None]])
        marks = jnp.pad(marks, (0, mine - marks.shape[0])).astype(BF)[None]

    places = jnp.stack([iy, ix, ik, ik, iz]).astype(jnp.int32)
    aligned = share % 128 == 0
    with jax.named_scope("spread_features"):
        if aligned:
            tile_shape = jax.ShapeDtypeStruct((cols, rows, mine), BF)
            *tiles, brims = call(
                partial(pack_kernel, share),
                "pack",
                0,
                [SMEM, VMEM, VMEM],
                [tile_shape] * 4 + [jax.ShapeDtypeStruct((4, cols, RIM, mine), BF)],
                [],
                [places, feature_map, marks],
            )
        else:
            packed = feature_map.transpose(1, 0, 2).reshape(cols, rows, zs, 2, 2, share)
            packed = packed.transpose(3, 4, 0, 1, 2, 5)
            packed = packed.reshape(4, cols, rows, mine)
            tiles = [
                lax.dynamic_index_in_dim(packed, (iy ^ dy) * 2 + (ix ^ dx), 0, False)
                for dy in range(2)
                for dx in range(2)
            ]
            brims = pick(packed[:, :, :REACH], packed[:, :, rows - REACH :], iy)
            brims = jnp.pad(brims, ((0, 0), (0, 0), (0, RIM - REACH), (0, 0)))
            brims = brims.at[:, :, REACH].set(marks)
        note = jnp.broadcast_to(marks[None, None], (4, cols, 1, mine))
        own, to_x, to_y, to_d = tiles
        mains = [own, swap(to_x, "x"), swap(to_y, "y"), crossed(to_d)]
        halo, mains = lax.optimization_barrier((beyond(brims, 0, 0), mains))
        halo = lax.dynamic_update_slice_in_dim(halo, note, REACH + 1, axis=2)
        halo = lax.all_to_all(halo, ("y", "x"), 0, 0)
        halos = [halo, swap(halo, "k")]

    mains = mains + [swap(g, "k") for g in mains]
    with jax.named_scope("marks"):
        told = jnp.stack([h[:, 0, REACH : REACH + 2] for h in halos]).astype(jnp.int32)
        told = told.reshape(2, 2, 2, 2, mine)
        strips = jnp.max(told[:, :, :, 1, :rows], axis=(0, 2))
        edges = jnp.max(told[:, :, :, 0, rows : rows + REACH], axis=(0, 2))
        cut = jnp.sum(told[:, 0, :, 1, rows + REACH])
        strip_plane = strips.reshape(2 * rows)
        top, bottom = edges[1], edges[0]
        strip_tall = jnp.concatenate([top, strip_plane, bottom])
        masks = jnp.stack(
            [
                jnp.stack(
                    [
                        strip_plane
                        == lax.slice_in_dim(strip_tall, REACH + s * d, REACH + s * d + 2 * rows)
                        for s in (-1, 1)
                    ]
                )
                for d in spreads
            ]
        )
        masks = jnp.broadcast_to(masks[..., None], (3, 2, 2 * rows, 128)).astype(BF)
        info = jnp.stack([iy, ix, ik, cut, iz]).astype(jnp.int32)


    local_ids = image_ids.T.reshape(pixels)
    image_range = jnp.arange(images, dtype=jnp.int32)
    table = local_ids[:, None] == image_range[None, :]

    point_view = point_weight.reshape(zs, 2, 2, share, feat)
    atrous_view = atrous_weight.reshape(3, 3, 3, zs, 2, 2, share, feat)

    def forward(units):
        shape = (2, cols, rows, feat)
        return call(
            partial(forward_kernel, units, spreads, mine),
            "forward_taps",
            2 * 2048 * mine * 256 * 15,
            [SMEM] + [ANY] * 8 + [VMEM] * 3 + [ANY] * 2,
            [jax.ShapeDtypeStruct(shape, F32), jax.ShapeDtypeStruct(shape, BF)] * 2,
            [
                pltpu.VMEM((32 + 2 * REACH, 2 * PAD + 128, mine), BF),
                pltpu.VMEM((zs, share, feat), BF),
                pltpu.VMEM((2, 3, 3, zs, share, feat), BF),
                pltpu.VMEM((8, 128, feat), F32),
                pltpu.SemaphoreType.DMA((16,)),
                pltpu.SemaphoreType.DMA((2, 9)),
            ],
            [info, *mains, *halos, masks, point_view, atrous_view],
        )

    def reduce_first(parts):
        keep_x, send_x, keep_y, send_y = parts
        return keep_x, swap(send_x, "x"), keep_y, swap(send_y, "y")

    def reduce_middle(parts):
        keep_x, got_x, keep_y, got_y = parts
        more_x = (keep_x[1] + got_x[1].astype(F32)).astype(BF)
        more_y = (keep_y[1] + got_y[1].astype(F32)).astype(BF)
        return more_x, more_y

    def reduce_last(parts, last_x, last_y):
        keep_x, got_x, keep_y, got_y = parts
        value_x = keep_x[0] + got_x[0].astype(F32) + last_x.astype(F32)
        value_y = keep_y[0] + got_y[0].astype(F32) + last_y.astype(F32)
        return [value_x.reshape(pixels, feat), value_y.reshape(pixels, feat)]

    early = forward([None, 0])
    early_got = reduce_first(early)
    late = forward([1, 2])
    early_got, late = lax.optimization_barrier((early_got, late))
    late_got = reduce_first(late)
    early_more = reduce_middle(early_got)
    early_last = [swap(early_more[0], "y"), swap(early_more[1], "x")]

    half = share // 2
    strip_table = strip_plane[:, None] == image_range[None, :]
    with jax.named_scope("across"):
        mains_late, early_last = lax.optimization_barrier((mains, early_last))
        if aligned:
            across, row_sums, zero_sums = call(
                partial(across_kernel, share),
                "across",
                2 * 10**9,
                [SMEM] + [ANY] * 8,
                [
                    jax.ShapeDtypeStruct((mine // 2, 32 * 2 * rows), BF),
                    jax.ShapeDtypeStruct((2 * rows, mine), F32),
                    jax.ShapeDtypeStruct((1, mine), F32),
                ],
                [
                    pltpu.VMEM((32 + 2 * REACH, 2 * PAD + 128, mine), BF),
                    pltpu.VMEM((2, 2 * rows, mine), F32),
                    pltpu.SemaphoreType.DMA((16,)),
                ],
                [info, *mains_late],
            )
        else:
            columns = []
            for x in range(2):
                for k in range(2):
                    index = [(ik ^ k) * 4 + (iy ^ y) * 2 + (ix ^ x) for y in range(2)]
                    stack = [lax.select_n(n.astype(jnp.int32), *mains_late) for n in index]
                    columns.append(jnp.concatenate(stack, axis=1))
            plane = jnp.concatenate(columns, axis=0)
            in_strip = (jnp.arange(32) >= cut)[:, None, None]
            row_sums = jnp.sum(jnp.where(in_strip, plane.astype(F32), 0.0), axis=0)
            zero_sums = jnp.sum(jnp.where(in_strip, 0.0, plane.astype(F32)), axis=(0, 1))[None]
            plane = plane.reshape(32, 2 * rows, zs, 2, half)
            plane = lax.dynamic_index_in_dim(plane, ik, 3, False)
            across = plane.reshape(32 * 2 * rows, mine // 2).T

    with jax.named_scope("image_sums"):
        sums = lax.dot_general(
            strip_table.astype(F32),
            row_sums,
            (((0,), (0,)), ((), ())),
            precision=lax.Precision.HIGHEST,
        )
        sums = jnp.where(image_range[:, None] == 0, zero_sums, sums)
        pool_mine = pool_weight.reshape(zs, 2, 2, share, feat)
        pool_mine = lax.dynamic_slice(
            pool_mine, (0, iy, ix, 0, 0), (zs, 1, 1, share, feat)
        ).reshape(mine, feat)
        per_image_part = 0.5 * exact(sums, pool_mine.astype(F32))
        strip_rows = jnp.sum(strip_table.astype(F32), axis=0)
        strip_rows = jnp.where((iy == 0) & (ix == 0) & (ik == 0), strip_rows, 0.0)
        strip_rows = jnp.pad(strip_rows, (0, -images % feat)).reshape(-1, feat)

    late_got, across, sums = lax.optimization_barrier((late_got, across, sums))
    late_more = reduce_middle(late_got)
    branches = reduce_last(early_got, *early_last)
    branches += reduce_last(late_got, swap(late_more[0], "y"), swap(late_more[1], "x"))

    first = jnp.concatenate([moments(value) for value in branches], axis=0)
    first = allsum(jnp.concatenate([first, per_image_part, strip_rows], axis=0))
    strip_rows = first[8 + images :].reshape(-1)[:images]
    counts = jnp.where(
        image_range == 0,
        (cut * (rows * row_count)).astype(F32),
        strip_rows * (4 * cols - cut).astype(F32),
    )
    per_image = first[8 : 8 + images] / counts[:, None]
    first = first[:8].reshape(4, 2, feat).transpose(1, 0, 2).reshape(2, 4 * feat)
    weighted = counts[:, None] * per_image
    pool_stats = jnp.stack([jnp.sum(weighted, axis=0), jnp.sum(weighted * per_image, axis=0)])
    four = 4 * feat
    flat_gain, flat_shift = bn_gain[:4].reshape(four), bn_shift[:4].reshape(four)
    mean = first[0] / total
    scale = lax.rsqrt(first[1] / total - mean * mean + EPSILON)
    normed = (jnp.concatenate(branches, axis=1) - mean) * scale
    lifted = normed * flat_gain + flat_shift
    mean4 = pool_stats[0] / total
    scale4 = lax.rsqrt(pool_stats[1] / total - mean4 * mean4 + EPSILON)
    normed4 = (per_image - mean4) * scale4
    lifted4 = normed4 * bn_gain[4] + bn_shift[4]
    joined = smooth(lifted).astype(BF)
    joined4 = smooth(lifted4).astype(BF)
    table_float = table.astype(F32)
    head = dot(joined, project_weight[:four]) + exact(
        table_float, dot(joined4, project_weight[four:])
    )
    head_stats = allsum(moments(head))
    head_mean = head_stats[0] / total
    head_scale = lax.rsqrt(head_stats[1] / total - head_mean * head_mean + EPSILON)
    head_norm = (head - head_mean) * head_scale
    head_lift = head_norm * bn_gain[5] + bn_shift[5]
    output = smooth(head_lift).astype(BF).reshape(cols, rows, feat)
    cotangent = out_grad.transpose(1, 0, 2).reshape(pixels, feat).astype(F32)
    head_grad = cotangent * smooth_slope(head_lift)
    head_back = allsum(
        jnp.stack([jnp.sum(head_grad, axis=0), jnp.sum(head_grad * head_norm, axis=0)])
    )
    head_slope = (
        bn_gain[5]
        * head_scale
        * (head_grad - head_back[0] / total - head_norm * head_back[1] / total)
    ).astype(BF)
    joined_grad = lax.dot_general(
        head_slope, project_weight[:four], (((1,), (1,)), ((), ())), preferred_element_type=F32
    )
    grads = joined_grad * smooth_slope(lifted)
    image_heads = jnp.einsum(
        "pi,pf->if", table.astype(BF), head_slope, preferred_element_type=F32
    )
    rear = jnp.concatenate(
        [
            jnp.stack([jnp.sum(grads, axis=0), jnp.sum(grads * normed, axis=0)]).reshape(8, feat),
            image_heads,
        ],
        axis=0,
    )
    rear = allsum(rear)
    shift_back, gain_back = rear[:4].reshape(four), rear[4:8].reshape(four)
    slopes = (
        flat_gain * scale * (grads - shift_back / total - normed * gain_back / total)
    ).astype(BF)

    with jax.named_scope("project_grad"):
        project_inputs = joined, head_slope

    with jax.named_scope("spread_slopes"):
        point_tile, *tiles_out = [
            slopes[:, k * feat : (k + 1) * feat].reshape(cols, rows, feat) for k in range(4)
        ]
        brim = beyond(rim(tiles_out[0], 16), 0, 0)
        deep = rim(tiles_out[2], 32)
        brims = jnp.concatenate([rim(tiles_out[1], 16), deep[:, :16], deep[:, 16:]], axis=2)
        brims = beyond(brims, 0, 0)

        def both_cores(got):
            return got + [swap(g, "k") for g in got]

        tile3 = jnp.concatenate([tiles_out[0], brim], axis=1)
        got3 = [tile3, swap(tile3, "x"), swap(tile3, "y"), crossed(tile3)]
        left, right = gate(project_inputs, tile3)
        project_part = lax.dot_general(
            left, right, (((0,), (0,)), ((), ())), preferred_element_type=F32
        )
        blocks = project_part.astype(BF).reshape(4, feat, feat)
        blocks = lax.all_to_all(blocks, ("x", "k"), 0, 0)
        across, blocks = lax.optimization_barrier((across, blocks))
        project_sum = jnp.sum(blocks.astype(F32), axis=0)
        project_low = project_sum.astype(BF)
        project_got = z_swap(project_low, 1)
        got3, brims = lax.optimization_barrier((got3, brims))
        edges = [brims[:, :, i * feat : (i + 1) * feat] for i in range(3)]
        tile2 = jnp.concatenate([tiles_out[1], edges[0]], axis=1)
        tile1 = jnp.concatenate([tiles_out[2], edges[1], edges[2], point_tile], axis=1)
        group3 = both_cores(got3)
        tile2, group3, output = lax.optimization_barrier((tile2, group3, output))
        output = output.transpose(1, 0, 2)
        arrived2 = [tile2, swap(tile2, "x"), swap(tile2, "y"), crossed(tile2)]

    rear, sums = gate((rear, sums), tile3)
    image_heads = rear[8:]
    grads4 = smooth_slope(lifted4) * exact(image_heads, project_weight[four:].astype(F32).T)
    shift4, gain4 = jnp.sum(grads4, axis=0), jnp.sum(grads4 * normed4, axis=0)
    image_slope = (
        bn_gain[4]
        * scale4
        * (grads4 - counts[:, None] * (shift4 / total + normed4 * gain4 / total))
    )
    image_low = image_slope.astype(BF)
    spread_back = (
        lax.dot_general(
            image_low, pool_mine, (((1,), (1,)), ((), ())), preferred_element_type=F32
        )
        / counts[:, None]
    )
    strip_back = exact(strip_table.astype(F32), spread_back)
    sums_mine = lax.dynamic_index_in_dim(sums.reshape(images, zs, 2, half), ik, 2, False)
    pool_part = lax.dot_general(
        sums_mine.reshape(images, mine // 2),
        image_low.astype(F32) / counts[:, None],
        (((0,), (0,)), ((), ())),
        precision=lax.Precision.HIGHEST,
    )

    def weight_grad(b, tiles, lanes_at, more=()):
        taps = 8 + len(lanes_at) + len(more)
        return call(
            partial(weight_kernel, spreads[b], b, lanes_at, feat),
            "weight_taps",
            2 * 4096 * (mine // 2) * 256 * 15,
            [SMEM] + [ANY] * 8 + [VMEM] * (2 + len(more)),
            [jax.ShapeDtypeStruct((2, taps, half, feat), BF)] * 2
            if zs == 4
            else [jax.ShapeDtypeStruct((zs, taps, half, feat), BF)],
            [
                pltpu.VMEM((len(lanes_at), 32 + 2 * REACH, 2 * PAD + 128, feat), BF),
                pltpu.VMEM((zs, taps, half, feat), BF),
                pltpu.SemaphoreType.DMA((2, 16)),
                pltpu.SemaphoreType.DMA((4,)),
            ],
            [info, *tiles, masks, across, *more],
            out_specs=[ANY] * (2 if zs == 4 else 1),
        )

    def collect(pieces, first, buffer, pool=None):
        count = 9 if buffer else 18
        extras = [1, 1] if buffer else [pieces[0].shape[0] - count]
        grad = jax.ShapeDtypeStruct((27, 4, half, feat), F32)
        sides = [jax.ShapeDtypeStruct((4, n, half, feat), F32) for n in extras]
        if pool is not None:
            sides = [jax.ShapeDtypeStruct((5, *pool.shape), F32)]
        given = buffer if pool is None else [pool]
        return call(
            partial(collect_kernel, first, count, extras),
            "collect",
            6 * 10**9,
            [SMEM] + [VMEM] * 4 + [VMEM if pool is not None else ANY],
            [grad, *sides],
            [pltpu.VMEM((count, 4, half, feat), F32), pltpu.SemaphoreType.DMA],
            [places, *pieces, *given],
            out_specs=[ANY] + [VMEM] * len(extras),
            aliases={5: 0} if buffer else {},
        )

    def scatter_first(part):
        if zs != 4:
            return lax.psum_scatter(part[0], "z", scatter_dimension=0, tiled=True), None
        return part[0], z_swap(part[1], 1)

    def scatter_second(state):
        keep, got = state
        if zs != 4:
            return keep, None
        more = (keep[1].astype(F32) + got[1].astype(F32)).astype(BF)
        return keep[0].astype(F32) + got[0].astype(F32), z_swap(more, 3)

    def scatter_last(state):
        keep, got = state
        if zs != 4:
            return keep[0]
        return (keep + got.astype(F32)).astype(BF)

    across, pool_part, spread_back, strip_back = lax.optimization_barrier(
        (across, pool_part, spread_back, strip_back)
    )
    part3 = weight_grad(0, group3, [(0, 16)])
    arrived2, part3, project_got = lax.optimization_barrier((arrived2, part3, project_got))
    project_sum = project_low.astype(F32) + project_got.astype(F32)
    step = 2
    while step < zs // 2:
        project_sum = project_sum + z_swap(project_sum, step)
        step *= 2
    project_low = project_sum.astype(BF)
    project_got = z_swap(project_low, step)
    group2 = both_cores(arrived2)
    tile1, group2 = lax.optimization_barrier((tile1, group2))
    arrived1 = [tile1, swap(tile1, "x"), swap(tile1, "y"), crossed(tile1)]
    sums3 = scatter_first(part3)
    part2 = weight_grad(1, group2, [(0, 16)])
    part2, group2, project_got, sums3 = lax.optimization_barrier(
        (part2, group2, project_got, sums3)
    )
    sums2, sums3 = scatter_first(part2), scatter_second(sums3)
    project_low = (project_low.astype(F32) + project_got.astype(F32)).astype(BF)
    project_low = gate(project_low, part2)

    def input_part(chosen, groups, pointed, more, outs):
        n = len(chosen)
        scratch = [
            pltpu.VMEM((n, 32 + 2 * REACH, 2 * PAD + 128, feat), BF),
            pltpu.VMEM((n, 3, zs, share, 3 * feat), BF),
        ]
        if pointed:
            scratch += [pltpu.VMEM((zs, share, feat), BF), pltpu.VMEM((2, 8, 128, mine), F32)]
        scratch += [pltpu.SemaphoreType.DMA((n, 16)), pltpu.SemaphoreType.DMA((n, 9))]
        return call(
            partial(input_kernel, chosen, spreads, feat, pointed),
            "input_taps",
            2 * 2048 * mine * 256 * 20,
            [SMEM] + [ANY] * 8 * len(groups) + [VMEM] + [ANY] * 2 + [VMEM] * len(more),
            outs,
            scratch,
            [info, *[t for g in groups for t in g], masks, point_view, atrous_view, *more],
        )

    with jax.named_scope("input_grad"):
        sums_so_far = input_part(
            [(0, 0, 0, 16), (1, 1, 0, 16)],
            [group3, group2],
            False,
            [],
            jax.ShapeDtypeStruct((2, cols, 2 * rows, mine), F32),
        )
    arrived1, sums_so_far, sums2, sums3 = lax.optimization_barrier(
        (arrived1, sums_so_far, sums2, sums3)
    )
    group1 = both_cores(arrived1)
    sums2 = scatter_second(sums2)
    project_got = swap(gate(project_low, arrived1), "y")
    part1 = weight_grad(2, group1, [(0, 32), (96, 0)], [pool_part])
    sums3, sums2, project_got, part1 = lax.optimization_barrier(
        (sums3, sums2, project_got, part1)
    )
    project_sum = project_low.astype(F32) + project_got.astype(F32)
    project_sum = project_sum.astype(BF).reshape(feat // half, half, feat)
    joint = jnp.concatenate([scatter_last(sums3), scatter_last(sums2), project_sum], axis=0)
    joint_x = swap(joint, "x")
    sums1 = scatter_first(part1)
    with jax.named_scope("input_grad"):
        group1, part1 = lax.optimization_barrier((group1, part1))
        shape = jax.ShapeDtypeStruct((cols, rows, mine), BF)
        own, to_x, to_y, to_d = input_part(
            [(2, 0, 0, 32), (None, 0, 96, 0)],
            [group1],
            True,
            [sums_so_far, spread_back[:1], strip_back],
            [shape] * 4,
        )
        sums1, joint_x = gate((sums1, joint_x), own)
        got = [own, swap(to_x, "x"), swap(to_y, "y"), crossed(to_d)]
        sums1 = scatter_second(sums1)
        joint, joint_x = lax.optimization_barrier((joint, joint_x))
        pieces32 = [joint, swap(joint, "k"), joint_x, swap(joint_x, "k")]
        project_pool = lax.dot_general(
            joined4.astype(F32),
            image_heads,
            (((0,), (0,)), ((), ())),
            precision=lax.Precision.HIGHEST,
        ).reshape(feat // half, half, feat)
        grad, project_grad = collect(pieces32, 0, [], project_pool)
        project_grad = project_grad.reshape(5 * feat, feat)
        got, sums1, grad = lax.optimization_barrier((got, sums1, grad))
        if aligned:
            input_grad = call(
                partial(unpack_kernel, share),
                "unpack",
                4 * 10**9,
                [SMEM] + [VMEM] * 4,
                jax.ShapeDtypeStruct((rows, cols, chans), BF),
                [],
                [places, *got],
            )
        else:
            planes = []
            for y in range(2):
                for x in range(2):
                    index = ((iy ^ y) * 2 + (ix ^ x)).astype(jnp.int32)
                    planes.append(lax.select_n(index, *got).reshape(cols, rows, zs, share))
            input_grad = jnp.stack(planes, axis=3).reshape(cols, rows, chans).transpose(1, 0, 2)

    done = scatter_last(sums1)
    done_x = swap(done, "x")
    done_x, grad, input_grad = lax.optimization_barrier((done_x, grad, input_grad))
    pieces1 = [done, swap(done, "k"), done_x, swap(done_x, "k")]
    grad, point_grad, pool_grad = collect(pieces1, 18, [grad])
    atrous_grad = grad.reshape(3, 3, 3, 4 * half, feat)
    point_grad, pool_grad = (v.reshape(4 * half, feat) for v in (point_grad, pool_grad))

    gain_grad = jnp.concatenate([rear[4:8], gain4[None], head_back[1][None]], axis=0)
    shift_grad = jnp.concatenate([rear[:4], shift4[None], head_back[0][None]], axis=0)
    return (
        output,
        input_grad,
        point_grad,
        atrous_grad,
        pool_grad,
        project_grad,
        gain_grad,
        shift_grad,
    )


def solution(mesh):
    row, col = mesh.devices.shape
    fine = Mesh(mesh.devices.reshape(row // 2, 2, col // 2, 2), ("z", "y", "x", "k"))
    rows, cols = ("z", "y"), ("x", "k")
    placed = (
        P(rows, cols, None),
        P(rows, cols),
        P(),
        P(),
        P(),
        P(),
        P(),
        P(),
        P(rows, cols, None),
    )
    return jax.shard_map(
        per_device,
        mesh=fine,
        in_specs=placed,
        out_specs=(
            P(rows, cols, None),
            P(rows, cols, None),
            P(rows, None),
            P(None, None, None, rows, None),
            P(rows, None),
            P(),
            P(),
            P(),
        ),
        check_vma=False,
    )
```

profile of v0, /device:TPU:0, one launch (start us, length us, event | category | flops | bytes accessed | tf_op | source)
XLA Modules:
  0.0 363.7 jit_solution(12061796240054342139)
XLA Ops:
  4.9 4.3 %pack.1 = (bf16[8,64,512]{2,1,0:T(8,128)(2,1)}, bf16[8,64,512]{2,1,0:T(8,128)(2,1)}, bf16[8,64,512]{2,1,0:T(8,128)(2,1)}, bf16[8,64,512]{2,1,0:T(8,128)(2,1)}, bf16[4,8,24,512]{3,2,1,0:T(8,128)(2,1)}) custom-call(s32[5]{0:T(128)} %stack.127.info, bf16[64,8,2048]{2,1,0:T(8,128)(2,1)} %full.1, bf16[1,512]{1,0:T(2,128)(2,1)} %broadcast_in_dim.38.marks), custom_call_target="tpu_custom_call" | custom-call | bytes 10000000 | tf_op jit(solution)/shard_map/spread_features/pack/pallas_call | solution.py:482
  13.6 3.8 %collective-permute-start.2 = (bf16[8,64,512]{2,1,0:T(8,128)(2,1)}, bf16[8,64,512]{2,1,0:T(8,128)(2,1)}, u32[]{:S(2)}, u32[]{:S(2)}) collective-permute-start(bf16[8,64,512]{2,1,0:T(8,128)(2,1)} %get-tuple-element.166), channel_id=1, source_target_pairs={{0,4},{4,0},{1,5},{5,1},{2,6},{6,2},{3,7},{7,3},{8,12},{12,8},{9,1... | collective-permute-start | bytes 1572872 | tf_op jit(solution)/shard_map/spread_features/ppermute | solution.py:34
  17.4 9.2 %collective-permute-done.1.refs_1_ = bf16[8,64,512]{2,1,0:T(8,128)(2,1)} collective-permute-done((bf16[8,64,512]{2,1,0:T(8,128)(2,1)}, bf16[8,64,512]{2,1,0:T(8,128)(2,1)}, u32[]{:S(2)}, u32[]{:S(2)}) %collective-permute-start.1) | collective-permute-done | bytes 524320 | tf_op jit(solution)/shard_map/spread_features/ppermute | solution.py:34
  26.7 13.0 %collective-permute-done.2.refs_2_ = bf16[8,64,512]{2,1,0:T(8,128)(2,1)} collective-permute-done((bf16[8,64,512]{2,1,0:T(8,128)(2,1)}, bf16[8,64,512]{2,1,0:T(8,128)(2,1)}, u32[]{:S(2)}, u32[]{:S(2)}) %collective-permute-start.2) | collective-permute-done | bytes 524320 | tf_op jit(solution)/shard_map/spread_features/ppermute | solution.py:34
  41.0 13.1 %all_to_all.10.refs_8_ = bf16[4,8,24,512]{3,2,1,0:T(8,128)(2,1)S(1)} all-to-all(bf16[4,8,24,512]{3,2,1,0:T(8,128)(2,1)S(1)} %dynamic_update_slice.3), channel_id=1, replica_groups=mesh['z'=4,'y'=2,'x'=2,'k'=2] {'y','x'}, dimensions={0} | all-to-all | bytes 1572864 | tf_op jit(solution)/shard_map/spread_features/all_to_all | solution.py:573
  60.6 11.7 %forward_taps.2 = (f32[2,8,64,256]{3,2,1,0:T(8,128)}, bf16[2,8,64,256]{3,2,1,0:T(8,128)(2,1)}, f32[2,8,64,256]{3,2,1,0:T(8,128)}, bf16[2,8,64,256]{3,2,1,0:T(8,128)(2,1)}) custom-call(s32[5]{0:T(128)} %stack.132.info, bf16[8,64,512]{2,1,0:T(8,128)(2,1)} %get-tuple-element.191.refs_0_, bf16[8,64,512]{2,1,0:T(8,128)(2,1)} %collective-permute-done.1.refs_1_, ...), custom_call_target="tpu_custom_call" | custom-call | flops 8053063680 | bytes 10000000 | tf_op jit(solution)/shard_map/forward_taps/pallas_call | solution.py:482
  73.8 13.0 %forward_taps.3 = (f32[2,8,64,256]{3,2,1,0:T(8,128)}, bf16[2,8,64,256]{3,2,1,0:T(8,128)(2,1)}, f32[2,8,64,256]{3,2,1,0:T(8,128)}, bf16[2,8,64,256]{3,2,1,0:T(8,128)(2,1)}) custom-call(s32[5]{0:T(128)} %stack.132.info, bf16[8,64,512]{2,1,0:T(8,128)(2,1)} %get-tuple-element.191.refs_0_, bf16[8,64,512]{2,1,0:T(8,128)(2,1)} %collective-permute-done.1.refs_1_, ...), custom_call_target="tpu_custom_call" | custom-call | flops 8053063680 | bytes 10000000 | tf_op jit(solution)/shard_map/forward_taps/pallas_call | solution.py:482
  91.7 4.9 %collective-permute-done.12 = bf16[8,64,256]{2,1,0:T(8,128)(2,1)S(1)} collective-permute-done((bf16[8,64,256]{2,1,0:T(8,128)(2,1)S(1)}, bf16[8,64,256]{2,1,0:T(8,128)(2,1)S(1)}, u32[]{:S(2)}, u32[]{:S(2)}) %collective-permute-start.12) | collective-permute-done | bytes 262176 | tf_op jit(solution)/shard_map/ppermute | solution.py:34
  97.8 5.8 %across.1 = (bf16[256,4096]{1,0:T(8,128)(2,1)}, f32[128,512]{1,0:T(8,128)}, f32[1,512]{1,0:T(1,128)}) custom-call(s32[5]{0:T(128)} %stack.132.info, bf16[8,64,512]{2,1,0:T(8,128)(2,1)} %get-tuple-element.191.refs_0_, bf16[8,64,512]{2,1,0:T(8,128)(2,1)} %collective-permute-done.1.refs_1_, bf16[8,64,512]{2,1,0:T(8,128)(2,1)} %collective-permute-done.2.refs_2_, ...), custom_call_target="tpu_custom_call" | custom-call | flops 2000000000 | bytes 10000000 | tf_op jit(solution)/shard_map/across/across/pallas_call | solution.py:482
  169.8 3.4 fusion.86
  202.8 3.6 %all-to-all-start.1 = ((bf16[4,256,256]{2,1,0:T(8,128)(2,1)}), bf16[4,256,256]{2,1,0:T(8,128)(2,1)S(1)}, u32[]{:S(2)}, u32[]{:S(2)}) async-start(bf16[4,256,256]{2,1,0:T(8,128)(2,1)} %bitcast.73), calls=%async_computation.1 | async-start | bytes 1048576 | tf_op jit(solution)/shard_map/spread_slopes/all_to_all | solution.py:797
  210.4 4.3 %collective-permute-done.47.refs_2_ = bf16[8,80,256]{2,1,0:T(8,128)(2,1)} collective-permute-done((bf16[8,80,256]{2,1,0:T(8,128)(2,1)S(1)}, bf16[8,80,256]{2,1,0:T(8,128)(2,1)}, u32[]{:S(2)}, u32[]{:S(2)}) %collective-permute-start.47) | collective-permute-done | bytes 327712 | tf_op jit(solution)/shard_map/spread_slopes/ppermute | solution.py:34
  225.8 11.5 %weight_taps.3 = (bf16[2,9,64,256]{3,2,1,0:T(8,128)(2,1)}, bf16[2,9,64,256]{3,2,1,0:T(8,128)(2,1)}) custom-call(s32[5]{0:T(128)} %stack.132.info, bf16[8,80,256]{2,1,0:T(8,128)(2,1)} %copy-done.22, bf16[8,80,256]{2,1,0:T(8,128)(2,1)} %collective-permute-done.46.refs_1_, bf16[8,80,256]{2,1,0:T(8,128)(2,1)} %collective-permute-done.47.refs_2_, ...), custom_call_target="tpu_custom_call" | custom-call | flops 8053063680 | bytes 10000000 | tf_op jit(solution)/shard_map/weight_taps/pallas_call | solution.py:482
  245.2 10.2 %weight_taps.4 = (bf16[2,9,64,256]{3,2,1,0:T(8,128)(2,1)}, bf16[2,9,64,256]{3,2,1,0:T(8,128)(2,1)}) custom-call(s32[5]{0:T(128)} %stack.132.info, bf16[8,80,256]{2,1,0:T(8,128)(2,1)} %copy-done.23, bf16[8,80,256]{2,1,0:T(8,128)(2,1)} %copy-done.63, bf16[8,80,256]{2,1,0:T(8,128)(2,1)} %copy-done.62, bf16[8,80,256]{2,1,0:T(8,128)(2,1)} %copy-done.61, ...), custom_call_target="tpu_custom_call" | custom-call | flops 8053063680 | bytes 10000000 | tf_op jit(solution)/shard_map/weight_taps/pallas_call | solution.py:482
  260.8 14.9 %input_taps.2.refs_11_ = f32[2,8,128,512]{3,2,1,0:T(8,128)} custom-call(s32[5]{0:T(128)} %stack.132.info, bf16[8,80,256]{2,1,0:T(8,128)(2,1)} %copy-done.22, bf16[8,80,256]{2,1,0:T(8,128)(2,1)} %collective-permute-done.46.refs_1_, bf16[8,80,256]{2,1,0:T(8,128)(2,1)} %collective-permute-done.47.refs_2_, bf16[8,80,256]{2,1,0:T(8,128)(2,1)} %collective-permute-done.48.refs_3_, ...), custom_call_target="tpu_custom_call" | custom-call | flops 10737418240 | bytes 10000000 | tf_op jit(solution)/shard_map/input_grad/input_taps/pallas_call | solution.py:482
  275.8 4.0 %collective-permute-done.68 = bf16[9,64,256]{2,1,0:T(8,128)(2,1)S(1)} collective-permute-done((bf16[9,64,256]{2,1,0:T(8,128)(2,1)S(1)}, bf16[9,64,256]{2,1,0:T(8,128)(2,1)S(1)}, u32[]{:S(2)}, u32[]{:S(2)}) %collective-permute-start.68) | collective-permute-done | bytes 294944 | tf_op jit(solution)/shard_map/ppermute | solution.py:39
  286.9 11.1 %weight_taps.5 = (bf16[2,11,64,256]{3,2,1,0:T(8,128)(2,1)}, bf16[2,11,64,256]{3,2,1,0:T(8,128)(2,1)}) custom-call(s32[5]{0:T(128)} %stack.132.info, bf16[8,160,256]{2,1,0:T(8,128)(2,1)} %copy-done.16, bf16[8,160,256]{2,1,0:T(8,128)(2,1)} %collective-permute-done.62.refs_1_, bf16[8,160,256]{2,1,0:T(8,128)(2,1)} %collective-permute-done.63.refs_2_, ...), custom_call_target="tpu_custom_call" | custom-call | flops 8053063680 | bytes 10000000 | tf_op jit(solution)/shard_map/weight_taps/pallas_call | solution.py:482
  300.5 10.2 %input_taps.3 = (bf16[8,64,512]{2,1,0:T(8,128)(2,1)}, bf16[8,64,512]{2,1,0:T(8,128)(2,1)}, bf16[8,64,512]{2,1,0:T(8,128)(2,1)}, bf16[8,64,512]{2,1,0:T(8,128)(2,1)}) custom-call(s32[5]{0:T(128)} %stack.132.info, bf16[8,160,256]{2,1,0:T(8,128)(2,1)} %copy-done.16, bf16[8,160,256]{2,1,0:T(8,128)(2,1)} %collective-permute-done.62.refs_1_, ...), custom_call_target="tpu_custom_call" | custom-call | flops 10737418240 | bytes 10000000 | tf_op jit(solution)/shard_map/input_grad/input_taps/pallas_call | solution.py:482
  310.7 6.4 %collective-permute-done.79.refs_2_ = bf16[22,64,256]{2,1,0:T(8,128)(2,1)} collective-permute-done((bf16[22,64,256]{2,1,0:T(8,128)(2,1)S(1)}, bf16[22,64,256]{2,1,0:T(8,128)(2,1)}, u32[]{:S(2)}, u32[]{:S(2)}) %collective-permute-start.79) | collective-permute-done | bytes 720928 | tf_op jit(solution)/shard_map/ppermute | solution.py:34
  325.3 5.4 %collect.2 = (f32[27,4,64,256]{3,2,1,0:T(8,128)}, f32[5,4,64,256]{3,2,1,0:T(8,128)}) custom-call(s32[5]{0:T(128)} %stack.127.info, bf16[22,64,256]{2,1,0:T(8,128)(2,1)} %copy-done.14, bf16[22,64,256]{2,1,0:T(8,128)(2,1)} %copy-done.49, bf16[22,64,256]{2,1,0:T(8,128)(2,1)} %collective-permute-done.79.refs_2_, bf16[22,64,256]{2,1,0:T(8,128)(2,1)} %copy-done.50, ...), custom_call_target="tpu_custom_call" | custom-call | flops 6000000000 | bytes 10000000 | tf_op jit(solution)/shard_map/input_grad/collect/pallas_call | solution.py:482
  334.5 10.5 %collective-permute-done.77.refs_3_ = bf16[8,64,512]{2,1,0:T(8,128)(2,1)} collective-permute-done((bf16[8,64,512]{2,1,0:T(8,128)(2,1)}, bf16[8,64,512]{2,1,0:T(8,128)(2,1)}, u32[]{:S(2)}, u32[]{:S(2)}) %collective-permute-start.77) | collective-permute-done | bytes 524320 | tf_op jit(solution)/shard_map/input_grad/ppermute | solution.py:43
  346.2 3.6 unpack.1
  349.8 6.3 %collective-permute-done.83.refs_2_ = bf16[11,64,256]{2,1,0:T(8,128)(2,1)S(1)} collective-permute-done((bf16[11,64,256]{2,1,0:T(8,128)(2,1)S(1)}, bf16[11,64,256]{2,1,0:T(8,128)(2,1)S(1)}, u32[]{:S(2)}, u32[]{:S(2)}) %collective-permute-start.83) | collective-permute-done | bytes 360480 | tf_op jit(solution)/shard_map/ppermute | solution.py:34
  359.7 3.8 %collect.3 = (f32[27,4,64,256]{3,2,1,0:T(8,128)}, f32[4,1,64,256]{3,2,1,0:T(8,128)}, f32[4,1,64,256]{3,2,1,0:T(8,128)}) custom-call(s32[5]{0:T(128)} %stack.127.info, bf16[11,64,256]{2,1,0:T(8,128)(2,1)} %copy-done.21, bf16[11,64,256]{2,1,0:T(8,128)(2,1)} %copy-done.55, bf16[11,64,256]{2,1,0:T(8,128)(2,1)} %copy-done.56, ...), custom_call_target="tpu_custom_call", output_to_operand_aliasing={{0}: (5, {})} | custom-call | flops 6000000000 | bytes 10000000 | tf_op jit(solution)/shard_map/collect/pallas_call | solution.py:482
  (419 shorter events, 171.8 us)
Async XLA Ops:
  9.2 31.2 %collective-permute-start = (bf16[4,8,24,512]{3,2,1,0:T(8,128)(2,1)}, bf16[4,8,24,512]{3,2,1,0:T(8,128)(2,1)S(1)}, u32[]{:S(2)}, u32[]{:S(2)}) collective-permute-start(bf16[4,8,24,512]{3,2,1,0:T(8,128)(2,1)} %get-tuple-element.163), channel_id=1, source_target_pairs={{4,12},{6,14},{8,0},{10,2},{12,20},{14,22},{16,8},{18,10},{20,28},... | collective-permute-start | bytes 2359304 | tf_op jit(solution)/shard_map/spread_features/ppermute | solution.py:533
  10.6 16.1 %collective-permute-start.1 = (bf16[8,64,512]{2,1,0:T(8,128)(2,1)}, bf16[8,64,512]{2,1,0:T(8,128)(2,1)}, u32[]{:S(2)}, u32[]{:S(2)}) collective-permute-start(bf16[8,64,512]{2,1,0:T(8,128)(2,1)} %get-tuple-element.165), channel_id=1, source_target_pairs={{0,2},{2,0},{1,3},{3,1},{4,6},{6,4},{5,7},{7,5},{8,10},{10,8},{9,1... | collective-permute-start | bytes 1572872 | tf_op jit(solution)/shard_map/spread_features/ppermute | solution.py:34
  13.6 26.0 %collective-permute-start.2 = (bf16[8,64,512]{2,1,0:T(8,128)(2,1)}, bf16[8,64,512]{2,1,0:T(8,128)(2,1)}, u32[]{:S(2)}, u32[]{:S(2)}) collective-permute-start(bf16[8,64,512]{2,1,0:T(8,128)(2,1)} %get-tuple-element.166), channel_id=1, source_target_pairs={{0,4},{4,0},{1,5},{5,1},{2,6},{6,2},{3,7},{7,3},{8,12},{12,8},{9,1... | collective-permute-start | bytes 1572872 | tf_op jit(solution)/shard_map/spread_features/ppermute | solution.py:34
  17.4 22.9 %collective-permute-start.3 = (bf16[8,64,512]{2,1,0:T(8,128)(2,1)}, bf16[8,64,512]{2,1,0:T(8,128)(2,1)}, u32[]{:S(2)}, u32[]{:S(2)}) collective-permute-start(bf16[8,64,512]{2,1,0:T(8,128)(2,1)} %get-tuple-element.167), channel_id=1, source_target_pairs={{0,6},{2,4},{4,2},{6,0},{1,7},{3,5},{5,3},{7,1},{8,14},{10,12},{12... | collective-permute-start | bytes 1572872 | tf_op jit(solution)/shard_map/spread_features/ppermute | solution.py:43
  89.8 16.6 %collective-permute-start.13 = (bf16[2,8,64,256]{3,2,1,0:T(8,128)(2,1)}, bf16[2,8,64,256]{3,2,1,0:T(8,128)(2,1)}, u32[]{:S(2)}, u32[]{:S(2)}) collective-permute-start(bf16[2,8,64,256]{3,2,1,0:T(8,128)(2,1)} %get-tuple-element.188), channel_id=1, source_target_pairs={{0,2},{2,0},{1,3},{3,1},{4,6},{6,4},{5,7},{7,5},{8,10},{10,8},{9,1... | collective-permute-start | bytes 1572872 | tf_op jit(solution)/shard_map/ppermute | solution.py:34
  90.8 16.6 %collective-permute-start.14 = (bf16[2,8,64,256]{3,2,1,0:T(8,128)(2,1)}, bf16[2,8,64,256]{3,2,1,0:T(8,128)(2,1)}, u32[]{:S(2)}, u32[]{:S(2)}) collective-permute-start(bf16[2,8,64,256]{3,2,1,0:T(8,128)(2,1)} %get-tuple-element.190), channel_id=1, source_target_pairs={{0,4},{4,0},{1,5},{5,1},{2,6},{6,2},{3,7},{7,3},{8,12},{12,8},{9,1... | collective-permute-start | bytes 1572872 | tf_op jit(solution)/shard_map/ppermute | solution.py:34
  193.7 16.6 %collective-permute-start.49 = (bf16[8,16,768]{2,1,0:T(8,128)(2,1)}, bf16[8,16,768]{2,1,0:T(8,128)(2,1)}, u32[]{:S(2)}, u32[]{:S(2)}) collective-permute-start(bf16[8,16,768]{2,1,0:T(8,128)(2,1)} %pad_maximum_fusion.4), channel_id=1, source_target_pairs={{4,12},{6,14},{8,0},{10,2},{12,20},{14,22},{16,8},{18,10},{20,28},... | collective-permute-start | bytes 589832 | tf_op jit(solution)/shard_map/spread_slopes/ppermute | solution.py:533
  200.7 16.0 %collective-permute-start.46 = (bf16[8,80,256]{2,1,0:T(8,128)(2,1)S(1)}, bf16[8,80,256]{2,1,0:T(8,128)(2,1)}, u32[]{:S(2)}, u32[]{:S(2)}) collective-permute-start(bf16[8,80,256]{2,1,0:T(8,128)(2,1)S(1)} %pad_maximum_fusion.2.refs_0_), channel_id=1, source_target_pairs={{0,2},{2,0},{1,3},{3,1},{4,6},{6,4},{5,7},{7,5},{8,10},{10,8},{9,1... | collective-permute-start | bytes 983048 | tf_op jit(solution)/shard_map/spread_slopes/ppermute | solution.py:34
  202.8 18.1 %all-to-all-start.1 = ((bf16[4,256,256]{2,1,0:T(8,128)(2,1)}), bf16[4,256,256]{2,1,0:T(8,128)(2,1)S(1)}, u32[]{:S(2)}, u32[]{:S(2)}) async-start(bf16[4,256,256]{2,1,0:T(8,128)(2,1)} %bitcast.73), calls=%async_computation.1 | async-start | bytes 1048576 | tf_op jit(solution)/shard_map/spread_slopes/all_to_all | solution.py:797
  221.0 16.4 %collective-permute-start.57 = (bf16[256,256]{1,0:T(8,128)(2,1)S(1)}, bf16[256,256]{1,0:T(8,128)(2,1)S(1)}, u32[]{:S(2)}, u32[]{:S(2)}) collective-permute-start(bf16[256,256]{1,0:T(8,128)(2,1)S(1)} %reduce_sum.224), channel_id=1, source_target_pairs={{0,8},{8,0},{16,24},{24,16},{1,9},{9,1},{17,25},{25,17},{2,10},{10... | collective-permute-start | bytes 393224 | tf_op jit(solution)/shard_map/spread_slopes/ppermute | solution.py:39
  222.2 15.1 %collective-permute-start.56 = (bf16[8,80,256]{2,1,0:T(8,128)(2,1)S(1)}, bf16[8,80,256]{2,1,0:T(8,128)(2,1)S(1)}, u32[]{:S(2)}, u32[]{:S(2)}) collective-permute-start(bf16[8,80,256]{2,1,0:T(8,128)(2,1)S(1)} %pad_maximum_fusion.3.refs_0_.refs_8_), channel_id=1, source_target_pairs={{0,6},{2,4},{4,2},{6,0},{1,7},{3,5},{5,3},{7,1},{8,14},{10,12},{12... | collective-permute-start | bytes 983048 | tf_op jit(solution)/shard_map/spread_slopes/ppermute | solution.py:43
  223.1 15.1 %collective-permute-start.55 = (bf16[8,80,256]{2,1,0:T(8,128)(2,1)S(1)}, bf16[8,80,256]{2,1,0:T(8,128)(2,1)S(1)}, u32[]{:S(2)}, u32[]{:S(2)}) collective-permute-start(bf16[8,80,256]{2,1,0:T(8,128)(2,1)S(1)} %pad_maximum_fusion.3.refs_0_.refs_8_), channel_id=1, source_target_pairs={{0,4},{4,0},{1,5},{5,1},{2,6},{6,2},{3,7},{7,3},{8,12},{12,8},{9,1... | collective-permute-start | bytes 983048 | tf_op jit(solution)/shard_map/spread_slopes/ppermute | solution.py:34
  239.4 16.0 %collective-permute-start.65 = (bf16[256,256]{1,0:T(8,128)(2,1)S(1)}, bf16[256,256]{1,0:T(8,128)(2,1)S(1)}, u32[]{:S(2)}, u32[]{:S(2)}) collective-permute-start(bf16[256,256]{1,0:T(8,128)(2,1)S(1)} %add_convert_fusion.12), channel_id=1, source_target_pairs={{0,16},{8,24},{16,0},{24,8},{1,17},{9,25},{17,1},{25,9},{2,18},{10... | collective-permute-start | bytes 393224 | tf_op jit(solution)/shard_map/ppermute | solution.py:39
  240.0 18.4 %collective-permute-start.66 = (bf16[2,9,64,256]{3,2,1,0:T(8,128)(2,1)}, bf16[2,9,64,256]{3,2,1,0:T(8,128)(2,1)S(1)}, u32[]{:S(2)}, u32[]{:S(2)}) collective-permute-start(bf16[2,9,64,256]{3,2,1,0:T(8,128)(2,1)} %get-tuple-element.249), channel_id=1, source_target_pairs={{0,8},{8,0},{16,24},{24,16},{1,9},{9,1},{17,25},{25,17},{2,10},{10... | collective-permute-start | bytes 1769480 | tf_op jit(solution)/shard_map/ppermute | solution.py:39
  241.7 38.1 %collective-permute-start.64 = (bf16[8,160,256]{2,1,0:T(8,128)(2,1)S(1)}, bf16[8,160,256]{2,1,0:T(8,128)(2,1)}, u32[]{:S(2)}, u32[]{:S(2)}) collective-permute-start(bf16[8,160,256]{2,1,0:T(8,128)(2,1)S(1)} %pad_maximum_fusion.1.refs_0_), channel_id=1, source_target_pairs={{0,6},{2,4},{4,2},{6,0},{1,7},{3,5},{5,3},{7,1},{8,14},{10,12},{12... | collective-permute-start | bytes 1966088 | tf_op jit(solution)/shard_map/ppermute | solution.py:43
  243.5 36.3 %collective-permute-start.63 = (bf16[8,160,256]{2,1,0:T(8,128)(2,1)S(1)}, bf16[8,160,256]{2,1,0:T(8,128)(2,1)}, u32[]{:S(2)}, u32[]{:S(2)}) collective-permute-start(bf16[8,160,256]{2,1,0:T(8,128)(2,1)S(1)} %pad_maximum_fusion.1.refs_0_), channel_id=1, source_target_pairs={{0,4},{4,0},{1,5},{5,1},{2,6},{6,2},{3,7},{7,3},{8,12},{12,8},{9,1... | collective-permute-start | bytes 1966088 | tf_op jit(solution)/shard_map/ppermute | solution.py:34
  244.3 35.5 %collective-permute-start.62 = (bf16[8,160,256]{2,1,0:T(8,128)(2,1)S(1)}, bf16[8,160,256]{2,1,0:T(8,128)(2,1)}, u32[]{:S(2)}, u32[]{:S(2)}) collective-permute-start(bf16[8,160,256]{2,1,0:T(8,128)(2,1)S(1)} %pad_maximum_fusion.1.refs_0_), channel_id=1, source_target_pairs={{0,2},{2,0},{1,3},{3,1},{4,6},{6,4},{5,7},{7,5},{8,10},{10,8},{9,1... | collective-permute-start | bytes 1966088 | tf_op jit(solution)/shard_map/ppermute | solution.py:34
  258.4 21.3 %collective-permute-start.67 = (bf16[2,9,64,256]{3,2,1,0:T(8,128)(2,1)}, bf16[2,9,64,256]{3,2,1,0:T(8,128)(2,1)S(1)}, u32[]{:S(2)}, u32[]{:S(2)}) collective-permute-start(bf16[2,9,64,256]{3,2,1,0:T(8,128)(2,1)} %get-tuple-element.259), channel_id=1, source_target_pairs={{0,8},{8,0},{16,24},{24,16},{1,9},{9,1},{17,25},{25,17},{2,10},{10... | collective-permute-start | bytes 1769480 | tf_op jit(solution)/shard_map/ppermute | solution.py:39
  258.6 21.1 %collective-permute-start.68 = (bf16[9,64,256]{2,1,0:T(8,128)(2,1)S(1)}, bf16[9,64,256]{2,1,0:T(8,128)(2,1)S(1)}, u32[]{:S(2)}, u32[]{:S(2)}) collective-permute-start(bf16[9,64,256]{2,1,0:T(8,128)(2,1)S(1)} %get-tuple-element.349), channel_id=1, source_target_pairs={{0,24},{8,16},{16,8},{24,0},{1,25},{9,17},{17,9},{25,1},{2,26},{10... | collective-permute-start | bytes 884744 | tf_op jit(solution)/shard_map/ppermute | solution.py:39
  282.2 15.8 %collective-permute-start.74 = (bf16[256,256]{1,0:T(8,128)(2,1)S(1)}, bf16[256,256]{1,0:T(8,128)(2,1)}, u32[]{:S(2)}, u32[]{:S(2)}) collective-permute-start(bf16[256,256]{1,0:T(8,128)(2,1)S(1)} %add_convert_fusion.11), channel_id=1, source_target_pairs={{0,4},{4,0},{1,5},{5,1},{2,6},{6,2},{3,7},{7,3},{8,12},{12,8},{9,1... | collective-permute-start | bytes 393224 | tf_op jit(solution)/shard_map/ppermute | solution.py:34
  299.0 18.1 %collective-permute-start.78 = (bf16[2,11,64,256]{3,2,1,0:T(8,128)(2,1)}, bf16[2,11,64,256]{3,2,1,0:T(8,128)(2,1)S(1)}, u32[]{:S(2)}, u32[]{:S(2)}) collective-permute-start(bf16[2,11,64,256]{3,2,1,0:T(8,128)(2,1)} %get-tuple-element.277), channel_id=1, source_target_pairs={{0,8},{8,0},{16,24},{24,16},{1,9},{9,1},{17,25},{25,17},{2,10},{10... | collective-permute-start | bytes 2162696 | tf_op jit(solution)/shard_map/ppermute | solution.py:39
  299.3 17.7 %collective-permute-start.79 = (bf16[22,64,256]{2,1,0:T(8,128)(2,1)S(1)}, bf16[22,64,256]{2,1,0:T(8,128)(2,1)}, u32[]{:S(2)}, u32[]{:S(2)}) collective-permute-start(bf16[22,64,256]{2,1,0:T(8,128)(2,1)S(1)} %pad_maximum_fusion.refs_0_), channel_id=1, source_target_pairs={{0,2},{2,0},{1,3},{3,1},{4,6},{6,4},{5,7},{7,5},{8,10},{10,8},{9,1... | collective-permute-start | bytes 2162696 | tf_op jit(solution)/shard_map/ppermute | solution.py:34
  320.7 24.4 %collective-permute-start.77 = (bf16[8,64,512]{2,1,0:T(8,128)(2,1)}, bf16[8,64,512]{2,1,0:T(8,128)(2,1)}, u32[]{:S(2)}, u32[]{:S(2)}) collective-permute-start(bf16[8,64,512]{2,1,0:T(8,128)(2,1)} %get-tuple-element.292), channel_id=1, source_target_pairs={{0,6},{2,4},{4,2},{6,0},{1,7},{3,5},{5,3},{7,1},{8,14},{10,12},{12... | collective-permute-start | bytes 1572872 | tf_op jit(solution)/shard_map/input_grad/ppermute | solution.py:43
  322.4 22.6 %collective-permute-start.80 = (bf16[11,64,256]{2,1,0:T(8,128)(2,1)S(1)}, bf16[11,64,256]{2,1,0:T(8,128)(2,1)S(1)}, u32[]{:S(2)}, u32[]{:S(2)}) collective-permute-start(bf16[11,64,256]{2,1,0:T(8,128)(2,1)S(1)} %get-tuple-element.345), channel_id=1, source_target_pairs={{0,24},{8,16},{16,8},{24,0},{1,25},{9,17},{17,9},{25,1},{2,26},{10... | collective-permute-start | bytes 1081352 | tf_op jit(solution)/shard_map/input_grad/ppermute | solution.py:39
  (130 other events, 1167.5 us)
where the time goes:
time: 367 us; the launch traced here: 364 us
  waiting for transfers between devices  110 us (30%)
  Pallas kernels  106 us (29%)
  starting transfers between devices  83.6 us (23%)
  other arithmetic  20.6 us (6%)
  matrix products  14.2 us (4%)
  blocking collectives  13.1 us (4%)
  local copies, waits for them, and re-layouts  12.8 us (3%)
  between operations  3.97 us (1%)
    pallas_call x12, Pallas kernels, call(): pl.pallas_call(kernel, name=name, in_specs=in_specs, out_specs=out_specs...  106 us
    ppermute x46, waiting for transfers between devices, swap(): return lax.ppermute(x, axis, SWAP)  62.6 us
    ppermute x46, starting transfers between devices, swap(): return lax.ppermute(x, axis, SWAP)  30.6 us
    ppermute x24, starting transfers between devices, quad(): lax.ppermute(x, axes, [(i, i ^ step) for i in range(4)])  29.3 us
    ppermute x24, waiting for transfers between devices, quad(): lax.ppermute(x, axes, [(i, i ^ step) for i in range(4)])  24.2 us
    all_to_all x1, blocking collectives, per_device(): halo = lax.all_to_all(halo, ('y', 'x'), 0, 0)  13.1 us
    ppermute x5, waiting for transfers between devices, crossed(): return lax.ppermute(x, ('y', 'x'), [(i, 3 - i) for i in range(4)])  11.3 us
    ppermute x8, starting transfers between devices, z_swap(): return lax.ppermute(x, 'z', [(i, i ^ step) for i in range(count)])  9.63 us
  transfers between devices with their start and end apart: 87, of which 49 were waited for; matrix products, arithmetic and copies ran while one was open for 6% of the time, Pallas kernels for 24%

commit v1 on v0

--- a/solution.py
+++ b/solution.py
@@ -970,7 +970,8 @@
         sums1, joint_x = gate((sums1, joint_x), own)
         got = [own, swap(to_x, "x"), swap(to_y, "y"), crossed(to_d)]
         sums1 = scatter_second(sums1)
-        joint, joint_x = lax.optimization_barrier((joint, joint_x))
+        got, sums1 = lax.optimization_barrier((got, sums1))
+        joint, joint_x = gate((joint, joint_x), got)
         pieces32 = [joint, swap(joint, "k"), joint_x, swap(joint_x, "k")]
         project_pool = lax.dot_general(
             joined4.astype(F32),
@@ -980,7 +981,6 @@
         ).reshape(feat // half, half, feat)
         grad, project_grad = collect(pieces32, 0, [], project_pool)
         project_grad = project_grad.reshape(5 * feat, feat)
-        got, sums1, grad = lax.optimization_barrier((got, sums1, grad))
         if aligned:
             input_grad = call(
                 partial(unpack_kernel, share),

time: 367 us -> 365 us (level)
  waiting for transfers between devices: 110 us -> 102 us
  Pallas kernels: 106 us -> 111 us
    pallas_call x12, Pallas kernels: 106 us -> 111 us  [call(): pl.pallas_call(kernel, name=name, in_specs=in_specs, out_specs=out_specs...]
    ppermute x46, waiting for transfers between devices: 62.6 us -> 57 us  [swap(): return lax.ppermute(x, axis, SWAP)]
  transfers between devices with their start and end apart: 87 -> 87, of which waited for: 49 -> 47; matrix products, arithmetic and copies ran while one was open for 6% -> 6% of each run, Pallas kernels for 24% -> 25%
where the time goes in v1:
time: 365 us; the launch traced here: 362 us
  Pallas kernels  111 us (30%)
  waiting for transfers between devices  102 us (28%)
  starting transfers between devices  84.6 us (23%)
  other arithmetic  21 us (6%)
  matrix products  14.2 us (4%)
  blocking collectives  13.1 us (4%)
  local copies, waits for them, and re-layouts  12.1 us (3%)
  between operations  3.93 us (1%)
    pallas_call x12, Pallas kernels, call(): pl.pallas_call(kernel, name=name, in_specs=in_specs, out_specs=out_specs...  111 us
    ppermute x46, waiting for transfers between devices, swap(): return lax.ppermute(x, axis, SWAP)  57 us
    ppermute x46, starting transfers between devices, swap(): return lax.ppermute(x, axis, SWAP)  31.1 us
    ppermute x24, starting transfers between devices, quad(): lax.ppermute(x, axes, [(i, i ^ step) for i in range(4)])  29.3 us
    ppermute x24, waiting for transfers between devices, quad(): lax.ppermute(x, axes, [(i, i ^ step) for i in range(4)])  24.2 us
    all_to_all x1, blocking collectives, per_device(): halo = lax.all_to_all(halo, ('y', 'x'), 0, 0)  13.1 us
    ppermute x5, waiting for transfers between devices, crossed(): return lax.ppermute(x, ('y', 'x'), [(i, 3 - i) for i in range(4)])  10.2 us
    ppermute x8, starting transfers between devices, z_swap(): return lax.ppermute(x, 'z', [(i, i ^ step) for i in range(count)])  10.1 us
  transfers between devices with their start and end apart: 87, of which 47 were waited for; matrix products, arithmetic and copies ran while one was open for 6% of the time, Pallas kernels for 25%

profile of v1, /device:TPU:0, one launch (start us, length us, event | category | flops | bytes accessed | tf_op | source)
XLA Modules:
  0.0 361.8 jit_solution(2198816275022069482)
XLA Ops:
  4.9 4.3 %pack.1 = (bf16[8,64,512]{2,1,0:T(8,128)(2,1)}, bf16[8,64,512]{2,1,0:T(8,128)(2,1)}, bf16[8,64,512]{2,1,0:T(8,128)(2,1)}, bf16[8,64,512]{2,1,0:T(8,128)(2,1)}, bf16[4,8,24,512]{3,2,1,0:T(8,128)(2,1)}) custom-call(s32[5]{0:T(128)} %stack.127.info, bf16[64,8,2048]{2,1,0:T(8,128)(2,1)} %full.1, bf16[1,512]{1,0:T(2,128)(2,1)} %broadcast_in_dim.38.marks), custom_call_target="tpu_custom_call" | custom-call | bytes 10000000 | tf_op jit(solution)/shard_map/spread_features/pack/pallas_call | solution.py:482
  10.6 3.0 collective-permute-start.1
  13.6 3.8 %collective-permute-start.2 = (bf16[8,64,512]{2,1,0:T(8,128)(2,1)}, bf16[8,64,512]{2,1,0:T(8,128)(2,1)}, u32[]{:S(2)}, u32[]{:S(2)}) collective-permute-start(bf16[8,64,512]{2,1,0:T(8,128)(2,1)} %get-tuple-element.165), channel_id=1, source_target_pairs={{0,4},{4,0},{1,5},{5,1},{2,6},{6,2},{3,7},{7,3},{8,12},{12,8},{9,1... | collective-permute-start | bytes 1572872 | tf_op jit(solution)/shard_map/spread_features/ppermute | solution.py:34
  17.4 9.2 %collective-permute-done.1.refs_1_ = bf16[8,64,512]{2,1,0:T(8,128)(2,1)} collective-permute-done((bf16[8,64,512]{2,1,0:T(8,128)(2,1)}, bf16[8,64,512]{2,1,0:T(8,128)(2,1)}, u32[]{:S(2)}, u32[]{:S(2)}) %collective-permute-start.1) | collective-permute-done | bytes 524320 | tf_op jit(solution)/shard_map/spread_features/ppermute | solution.py:34
  26.6 13.0 %collective-permute-done.2.refs_2_ = bf16[8,64,512]{2,1,0:T(8,128)(2,1)} collective-permute-done((bf16[8,64,512]{2,1,0:T(8,128)(2,1)}, bf16[8,64,512]{2,1,0:T(8,128)(2,1)}, u32[]{:S(2)}, u32[]{:S(2)}) %collective-permute-start.2) | collective-permute-done | bytes 524320 | tf_op jit(solution)/shard_map/spread_features/ppermute | solution.py:34
  41.0 13.1 %all_to_all.10.refs_8_ = bf16[4,8,24,512]{3,2,1,0:T(8,128)(2,1)S(1)} all-to-all(bf16[4,8,24,512]{3,2,1,0:T(8,128)(2,1)S(1)} %dynamic_update_slice.3), channel_id=1, replica_groups=mesh['z'=4,'y'=2,'x'=2,'k'=2] {'y','x'}, dimensions={0} | all-to-all | bytes 1572864 | tf_op jit(solution)/shard_map/spread_features/all_to_all | solution.py:573
  60.5 11.7 %forward_taps.2 = (f32[2,8,64,256]{3,2,1,0:T(8,128)}, bf16[2,8,64,256]{3,2,1,0:T(8,128)(2,1)}, f32[2,8,64,256]{3,2,1,0:T(8,128)}, bf16[2,8,64,256]{3,2,1,0:T(8,128)(2,1)}) custom-call(s32[5]{0:T(128)} %stack.132.info, bf16[8,64,512]{2,1,0:T(8,128)(2,1)} %get-tuple-element.190.refs_0_, bf16[8,64,512]{2,1,0:T(8,128)(2,1)} %collective-permute-done.1.refs_1_, ...), custom_call_target="tpu_custom_call" | custom-call | flops 8053063680 | bytes 10000000 | tf_op jit(solution)/shard_map/forward_taps/pallas_call | solution.py:482
  73.8 15.9 %forward_taps.3 = (f32[2,8,64,256]{3,2,1,0:T(8,128)}, bf16[2,8,64,256]{3,2,1,0:T(8,128)(2,1)}, f32[2,8,64,256]{3,2,1,0:T(8,128)}, bf16[2,8,64,256]{3,2,1,0:T(8,128)(2,1)}) custom-call(s32[5]{0:T(128)} %stack.132.info, bf16[8,64,512]{2,1,0:T(8,128)(2,1)} %get-tuple-element.190.refs_0_, bf16[8,64,512]{2,1,0:T(8,128)(2,1)} %collective-permute-done.1.refs_1_, ...), custom_call_target="tpu_custom_call" | custom-call | flops 8053063680 | bytes 10000000 | tf_op jit(solution)/shard_map/forward_taps/pallas_call | solution.py:482
  94.2 4.9 %collective-permute-done.12 = bf16[8,64,256]{2,1,0:T(8,128)(2,1)S(1)} collective-permute-done((bf16[8,64,256]{2,1,0:T(8,128)(2,1)S(1)}, bf16[8,64,256]{2,1,0:T(8,128)(2,1)S(1)}, u32[]{:S(2)}, u32[]{:S(2)}) %collective-permute-start.12) | collective-permute-done | bytes 262176 | tf_op jit(solution)/shard_map/ppermute | solution.py:34
  100.6 5.8 %across.1 = (bf16[256,4096]{1,0:T(8,128)(2,1)}, f32[128,512]{1,0:T(8,128)}, f32[1,512]{1,0:T(1,128)}) custom-call(s32[5]{0:T(128)} %stack.132.info, bf16[8,64,512]{2,1,0:T(8,128)(2,1)} %get-tuple-element.190.refs_0_, bf16[8,64,512]{2,1,0:T(8,128)(2,1)} %collective-permute-done.1.refs_1_, bf16[8,64,512]{2,1,0:T(8,128)(2,1)} %collective-permute-done.2.refs_2_, ...), custom_call_target="tpu_custom_call" | custom-call | flops 2000000000 | bytes 10000000 | tf_op jit(solution)/shard_map/across/across/pallas_call | solution.py:482
  171.6 3.4 fusion.86
  204.5 3.6 %all-to-all-start.1 = ((bf16[4,256,256]{2,1,0:T(8,128)(2,1)}), bf16[4,256,256]{2,1,0:T(8,128)(2,1)S(1)}, u32[]{:S(2)}, u32[]{:S(2)}) async-start(bf16[4,256,256]{2,1,0:T(8,128)(2,1)} %bitcast.73), calls=%async_computation.1 | async-start | bytes 1048576 | tf_op jit(solution)/shard_map/spread_slopes/all_to_all | solution.py:797
  212.1 4.4 %collective-permute-done.47.refs_2_ = bf16[8,80,256]{2,1,0:T(8,128)(2,1)} collective-permute-done((bf16[8,80,256]{2,1,0:T(8,128)(2,1)S(1)}, bf16[8,80,256]{2,1,0:T(8,128)(2,1)}, u32[]{:S(2)}, u32[]{:S(2)}) %collective-permute-start.47) | collective-permute-done | bytes 327712 | tf_op jit(solution)/shard_map/spread_slopes/ppermute | solution.py:34
  227.6 11.5 %weight_taps.3 = (bf16[2,9,64,256]{3,2,1,0:T(8,128)(2,1)}, bf16[2,9,64,256]{3,2,1,0:T(8,128)(2,1)}) custom-call(s32[5]{0:T(128)} %stack.132.info, bf16[8,80,256]{2,1,0:T(8,128)(2,1)} %copy-done.22, bf16[8,80,256]{2,1,0:T(8,128)(2,1)} %collective-permute-done.46.refs_1_, bf16[8,80,256]{2,1,0:T(8,128)(2,1)} %collective-permute-done.47.refs_2_, ...), custom_call_target="tpu_custom_call" | custom-call | flops 8053063680 | bytes 10000000 | tf_op jit(solution)/shard_map/weight_taps/pallas_call | solution.py:482
  247.0 10.2 %weight_taps.4 = (bf16[2,9,64,256]{3,2,1,0:T(8,128)(2,1)}, bf16[2,9,64,256]{3,2,1,0:T(8,128)(2,1)}) custom-call(s32[5]{0:T(128)} %stack.132.info, bf16[8,80,256]{2,1,0:T(8,128)(2,1)} %copy-done.23, bf16[8,80,256]{2,1,0:T(8,128)(2,1)} %copy-done.62, bf16[8,80,256]{2,1,0:T(8,128)(2,1)} %copy-done.61, bf16[8,80,256]{2,1,0:T(8,128)(2,1)} %copy-done.60, ...), custom_call_target="tpu_custom_call" | custom-call | flops 8053063680 | bytes 10000000 | tf_op jit(solution)/shard_map/weight_taps/pallas_call | solution.py:482
  257.3 3.0 collective-permute-done.66
  263.3 16.1 %input_taps.2.refs_11_ = f32[2,8,128,512]{3,2,1,0:T(8,128)} custom-call(s32[5]{0:T(128)} %stack.132.info, bf16[8,80,256]{2,1,0:T(8,128)(2,1)} %copy-done.22, bf16[8,80,256]{2,1,0:T(8,128)(2,1)} %collective-permute-done.46.refs_1_, bf16[8,80,256]{2,1,0:T(8,128)(2,1)} %collective-permute-done.47.refs_2_, bf16[8,80,256]{2,1,0:T(8,128)(2,1)} %collective-permute-done.48.refs_3_, ...), custom_call_target="tpu_custom_call" | custom-call | flops 10737418240 | bytes 10000000 | tf_op jit(solution)/shard_map/input_grad/input_taps/pallas_call | solution.py:482
  288.5 11.1 %weight_taps.5 = (bf16[2,11,64,256]{3,2,1,0:T(8,128)(2,1)}, bf16[2,11,64,256]{3,2,1,0:T(8,128)(2,1)}) custom-call(s32[5]{0:T(128)} %stack.132.info, bf16[8,160,256]{2,1,0:T(8,128)(2,1)} %copy-done.16, bf16[8,160,256]{2,1,0:T(8,128)(2,1)} %collective-permute-done.62.refs_1_, bf16[8,160,256]{2,1,0:T(8,128)(2,1)} %collective-permute-done.63.refs_2_, ...), custom_call_target="tpu_custom_call" | custom-call | flops 8053063680 | bytes 10000000 | tf_op jit(solution)/shard_map/weight_taps/pallas_call | solution.py:482
  302.4 12.0 %input_taps.3 = (bf16[8,64,512]{2,1,0:T(8,128)(2,1)}, bf16[8,64,512]{2,1,0:T(8,128)(2,1)}, bf16[8,64,512]{2,1,0:T(8,128)(2,1)}, bf16[8,64,512]{2,1,0:T(8,128)(2,1)}) custom-call(s32[5]{0:T(128)} %stack.132.info, bf16[8,160,256]{2,1,0:T(8,128)(2,1)} %copy-done.16, bf16[8,160,256]{2,1,0:T(8,128)(2,1)} %collective-permute-done.62.refs_1_, ...), custom_call_target="tpu_custom_call" | custom-call | flops 10737418240 | bytes 10000000 | tf_op jit(solution)/shard_map/input_grad/input_taps/pallas_call | solution.py:482
  322.4 9.2 %collective-permute-done.75.refs_1_ = bf16[8,64,512]{2,1,0:T(8,128)(2,1)S(1)} collective-permute-done((bf16[8,64,512]{2,1,0:T(8,128)(2,1)}, bf16[8,64,512]{2,1,0:T(8,128)(2,1)S(1)}, u32[]{:S(2)}, u32[]{:S(2)}) %collective-permute-start.75) | collective-permute-done | bytes 524320 | tf_op jit(solution)/shard_map/input_grad/ppermute | solution.py:34
  331.5 9.5 %collective-permute-done.77.refs_3_ = bf16[8,64,512]{2,1,0:T(8,128)(2,1)S(1)} collective-permute-done((bf16[8,64,512]{2,1,0:T(8,128)(2,1)}, bf16[8,64,512]{2,1,0:T(8,128)(2,1)S(1)}, u32[]{:S(2)}, u32[]{:S(2)}) %collective-permute-start.77) | collective-permute-done | bytes 524320 | tf_op jit(solution)/shard_map/input_grad/ppermute | solution.py:43
  343.8 3.6 unpack.1
  348.5 5.5 %collect.2 = (f32[27,4,64,256]{3,2,1,0:T(8,128)}, f32[5,4,64,256]{3,2,1,0:T(8,128)}) custom-call(s32[5]{0:T(128)} %stack.127.info, bf16[22,64,256]{2,1,0:T(8,128)(2,1)} %copy-done.14, bf16[22,64,256]{2,1,0:T(8,128)(2,1)} %copy-done.49, bf16[22,64,256]{2,1,0:T(8,128)(2,1)} %collective-permute-done.79.refs_2_, bf16[22,64,256]{2,1,0:T(8,128)(2,1)} %copy-done.50, ...), custom_call_target="tpu_custom_call" | custom-call | flops 6000000000 | bytes 10000000 | tf_op jit(solution)/shard_map/input_grad/collect/pallas_call | solution.py:482
  357.8 3.8 %collect.3 = (f32[27,4,64,256]{3,2,1,0:T(8,128)}, f32[4,1,64,256]{3,2,1,0:T(8,128)}, f32[4,1,64,256]{3,2,1,0:T(8,128)}) custom-call(s32[5]{0:T(128)} %stack.127.info, bf16[11,64,256]{2,1,0:T(8,128)(2,1)} %copy-done.21, bf16[11,64,256]{2,1,0:T(8,128)(2,1)} %copy-done.55, ...), custom_call_target="tpu_custom_call", output_to_operand_aliasing={{0}: (5, {})} | custom-call | flops 6000000000 | bytes 10000000 | tf_op jit(solution)/shard_map/collect/pallas_call | solution.py:482
  (417 shorter events, 166.4 us)
Async XLA Ops:
  9.2 31.2 %collective-permute-start = (bf16[4,8,24,512]{3,2,1,0:T(8,128)(2,1)}, bf16[4,8,24,512]{3,2,1,0:T(8,128)(2,1)S(1)}, u32[]{:S(2)}, u32[]{:S(2)}) collective-permute-start(bf16[4,8,24,512]{3,2,1,0:T(8,128)(2,1)} %get-tuple-element.162), channel_id=1, source_target_pairs={{4,12},{6,14},{8,0},{10,2},{12,20},{14,22},{16,8},{18,10},{20,28},... | collective-permute-start | bytes 2359304 | tf_op jit(solution)/shard_map/spread_features/ppermute | solution.py:533
  10.6 16.1 %collective-permute-start.1 = (bf16[8,64,512]{2,1,0:T(8,128)(2,1)}, bf16[8,64,512]{2,1,0:T(8,128)(2,1)}, u32[]{:S(2)}, u32[]{:S(2)}) collective-permute-start(bf16[8,64,512]{2,1,0:T(8,128)(2,1)} %get-tuple-element.164), channel_id=1, source_target_pairs={{0,2},{2,0},{1,3},{3,1},{4,6},{6,4},{5,7},{7,5},{8,10},{10,8},{9,1... | collective-permute-start | bytes 1572872 | tf_op jit(solution)/shard_map/spread_features/ppermute | solution.py:34
  13.6 26.0 %collective-permute-start.2 = (bf16[8,64,512]{2,1,0:T(8,128)(2,1)}, bf16[8,64,512]{2,1,0:T(8,128)(2,1)}, u32[]{:S(2)}, u32[]{:S(2)}) collective-permute-start(bf16[8,64,512]{2,1,0:T(8,128)(2,1)} %get-tuple-element.165), channel_id=1, source_target_pairs={{0,4},{4,0},{1,5},{5,1},{2,6},{6,2},{3,7},{7,3},{8,12},{12,8},{9,1... | collective-permute-start | bytes 1572872 | tf_op jit(solution)/shard_map/spread_features/ppermute | solution.py:34
  17.4 22.9 %collective-permute-start.3 = (bf16[8,64,512]{2,1,0:T(8,128)(2,1)}, bf16[8,64,512]{2,1,0:T(8,128)(2,1)}, u32[]{:S(2)}, u32[]{:S(2)}) collective-permute-start(bf16[8,64,512]{2,1,0:T(8,128)(2,1)} %get-tuple-element.166), channel_id=1, source_target_pairs={{0,6},{2,4},{4,2},{6,0},{1,7},{3,5},{5,3},{7,1},{8,14},{10,12},{12... | collective-permute-start | bytes 1572872 | tf_op jit(solution)/shard_map/spread_features/ppermute | solution.py:43
  72.2 17.4 %collective-permute-start.9 = (bf16[2,8,64,256]{3,2,1,0:T(8,128)(2,1)}, bf16[2,8,64,256]{3,2,1,0:T(8,128)(2,1)S(1)}, u32[]{:S(2)}, u32[]{:S(2)}) collective-permute-start(bf16[2,8,64,256]{3,2,1,0:T(8,128)(2,1)} %get-tuple-element.173), channel_id=1, source_target_pairs={{0,2},{2,0},{1,3},{3,1},{4,6},{6,4},{5,7},{7,5},{8,10},{10,8},{9,1... | collective-permute-start | bytes 1572872 | tf_op jit(solution)/shard_map/ppermute | solution.py:34
  73.2 16.4 %collective-permute-start.10 = (bf16[2,8,64,256]{3,2,1,0:T(8,128)(2,1)}, bf16[2,8,64,256]{3,2,1,0:T(8,128)(2,1)S(1)}, u32[]{:S(2)}, u32[]{:S(2)}) collective-permute-start(bf16[2,8,64,256]{3,2,1,0:T(8,128)(2,1)} %get-tuple-element.175), channel_id=1, source_target_pairs={{0,4},{4,0},{1,5},{5,1},{2,6},{6,2},{3,7},{7,3},{8,12},{12,8},{9,1... | collective-permute-start | bytes 1572872 | tf_op jit(solution)/shard_map/ppermute | solution.py:34
  92.6 16.6 %collective-permute-start.13 = (bf16[2,8,64,256]{3,2,1,0:T(8,128)(2,1)}, bf16[2,8,64,256]{3,2,1,0:T(8,128)(2,1)}, u32[]{:S(2)}, u32[]{:S(2)}) collective-permute-start(bf16[2,8,64,256]{3,2,1,0:T(8,128)(2,1)} %get-tuple-element.187), channel_id=1, source_target_pairs={{0,2},{2,0},{1,3},{3,1},{4,6},{6,4},{5,7},{7,5},{8,10},{10,8},{9,1... | collective-permute-start | bytes 1572872 | tf_op jit(solution)/shard_map/ppermute | solution.py:34
  195.5 16.6 %collective-permute-start.49 = (bf16[8,16,768]{2,1,0:T(8,128)(2,1)}, bf16[8,16,768]{2,1,0:T(8,128)(2,1)}, u32[]{:S(2)}, u32[]{:S(2)}) collective-permute-start(bf16[8,16,768]{2,1,0:T(8,128)(2,1)} %pad_maximum_fusion.4), channel_id=1, source_target_pairs={{4,12},{6,14},{8,0},{10,2},{12,20},{14,22},{16,8},{18,10},{20,28},... | collective-permute-start | bytes 589832 | tf_op jit(solution)/shard_map/spread_slopes/ppermute | solution.py:533
  202.6 16.0 %collective-permute-start.46 = (bf16[8,80,256]{2,1,0:T(8,128)(2,1)S(1)}, bf16[8,80,256]{2,1,0:T(8,128)(2,1)}, u32[]{:S(2)}, u32[]{:S(2)}) collective-permute-start(bf16[8,80,256]{2,1,0:T(8,128)(2,1)S(1)} %pad_maximum_fusion.2.refs_0_), channel_id=1, source_target_pairs={{0,2},{2,0},{1,3},{3,1},{4,6},{6,4},{5,7},{7,5},{8,10},{10,8},{9,1... | collective-permute-start | bytes 983048 | tf_op jit(solution)/shard_map/spread_slopes/ppermute | solution.py:34
  204.5 18.2 %all-to-all-start.1 = ((bf16[4,256,256]{2,1,0:T(8,128)(2,1)}), bf16[4,256,256]{2,1,0:T(8,128)(2,1)S(1)}, u32[]{:S(2)}, u32[]{:S(2)}) async-start(bf16[4,256,256]{2,1,0:T(8,128)(2,1)} %bitcast.73), calls=%async_computation.1 | async-start | bytes 1048576 | tf_op jit(solution)/shard_map/spread_slopes/all_to_all | solution.py:797
  222.8 16.3 %collective-permute-start.57 = (bf16[256,256]{1,0:T(8,128)(2,1)S(1)}, bf16[256,256]{1,0:T(8,128)(2,1)S(1)}, u32[]{:S(2)}, u32[]{:S(2)}) collective-permute-start(bf16[256,256]{1,0:T(8,128)(2,1)S(1)} %reduce_sum.224), channel_id=1, source_target_pairs={{0,8},{8,0},{16,24},{24,16},{1,9},{9,1},{17,25},{25,17},{2,10},{10... | collective-permute-start | bytes 393224 | tf_op jit(solution)/shard_map/spread_slopes/ppermute | solution.py:39
  241.2 16.0 %collective-permute-start.65 = (bf16[256,256]{1,0:T(8,128)(2,1)S(1)}, bf16[256,256]{1,0:T(8,128)(2,1)S(1)}, u32[]{:S(2)}, u32[]{:S(2)}) collective-permute-start(bf16[256,256]{1,0:T(8,128)(2,1)S(1)} %add_convert_fusion.12), channel_id=1, source_target_pairs={{0,16},{8,24},{16,0},{24,8},{1,17},{9,25},{17,1},{25,9},{2,18},{10... | collective-permute-start | bytes 393224 | tf_op jit(solution)/shard_map/ppermute | solution.py:39
  241.9 18.4 %collective-permute-start.66 = (bf16[2,9,64,256]{3,2,1,0:T(8,128)(2,1)}, bf16[2,9,64,256]{3,2,1,0:T(8,128)(2,1)S(1)}, u32[]{:S(2)}, u32[]{:S(2)}) collective-permute-start(bf16[2,9,64,256]{3,2,1,0:T(8,128)(2,1)} %get-tuple-element.248), channel_id=1, source_target_pairs={{0,8},{8,0},{16,24},{24,16},{1,9},{9,1},{17,25},{25,17},{2,10},{10... | collective-permute-start | bytes 1769480 | tf_op jit(solution)/shard_map/ppermute | solution.py:39
  243.5 38.1 %collective-permute-start.64 = (bf16[8,160,256]{2,1,0:T(8,128)(2,1)S(1)}, bf16[8,160,256]{2,1,0:T(8,128)(2,1)}, u32[]{:S(2)}, u32[]{:S(2)}) collective-permute-start(bf16[8,160,256]{2,1,0:T(8,128)(2,1)S(1)} %pad_maximum_fusion.1.refs_0_), channel_id=1, source_target_pairs={{0,6},{2,4},{4,2},{6,0},{1,7},{3,5},{5,3},{7,1},{8,14},{10,12},{12... | collective-permute-start | bytes 1966088 | tf_op jit(solution)/shard_map/ppermute | solution.py:43
  245.3 36.3 %collective-permute-start.63 = (bf16[8,160,256]{2,1,0:T(8,128)(2,1)S(1)}, bf16[8,160,256]{2,1,0:T(8,128)(2,1)}, u32[]{:S(2)}, u32[]{:S(2)}) collective-permute-start(bf16[8,160,256]{2,1,0:T(8,128)(2,1)S(1)} %pad_maximum_fusion.1.refs_0_), channel_id=1, source_target_pairs={{0,4},{4,0},{1,5},{5,1},{2,6},{6,2},{3,7},{7,3},{8,12},{12,8},{9,1... | collective-permute-start | bytes 1966088 | tf_op jit(solution)/shard_map/ppermute | solution.py:34
  246.1 35.5 %collective-permute-start.62 = (bf16[8,160,256]{2,1,0:T(8,128)(2,1)S(1)}, bf16[8,160,256]{2,1,0:T(8,128)(2,1)}, u32[]{:S(2)}, u32[]{:S(2)}) collective-permute-start(bf16[8,160,256]{2,1,0:T(8,128)(2,1)S(1)} %pad_maximum_fusion.1.refs_0_), channel_id=1, source_target_pairs={{0,2},{2,0},{1,3},{3,1},{4,6},{6,4},{5,7},{7,5},{8,10},{10,8},{9,1... | collective-permute-start | bytes 1966088 | tf_op jit(solution)/shard_map/ppermute | solution.py:34
  260.3 21.3 %collective-permute-start.67 = (bf16[2,9,64,256]{3,2,1,0:T(8,128)(2,1)}, bf16[2,9,64,256]{3,2,1,0:T(8,128)(2,1)S(1)}, u32[]{:S(2)}, u32[]{:S(2)}) collective-permute-start(bf16[2,9,64,256]{3,2,1,0:T(8,128)(2,1)} %get-tuple-element.258), channel_id=1, source_target_pairs={{0,8},{8,0},{16,24},{24,16},{1,9},{9,1},{17,25},{25,17},{2,10},{10... | collective-permute-start | bytes 1769480 | tf_op jit(solution)/shard_map/ppermute | solution.py:39
  261.1 20.4 %collective-permute-start.68 = (bf16[9,64,256]{2,1,0:T(8,128)(2,1)}, bf16[9,64,256]{2,1,0:T(8,128)(2,1)S(1)}, u32[]{:S(2)}, u32[]{:S(2)}) collective-permute-start(bf16[9,64,256]{2,1,0:T(8,128)(2,1)} %get-tuple-element.347), channel_id=1, source_target_pairs={{0,24},{8,16},{16,8},{24,0},{1,25},{9,17},{17,9},{25,1},{2,26},{10... | collective-permute-start | bytes 884744 | tf_op jit(solution)/shard_map/ppermute | solution.py:39
  299.7 20.7 %collective-permute-start.78 = (bf16[2,11,64,256]{3,2,1,0:T(8,128)(2,1)}, bf16[2,11,64,256]{3,2,1,0:T(8,128)(2,1)S(1)}, u32[]{:S(2)}, u32[]{:S(2)}) collective-permute-start(bf16[2,11,64,256]{3,2,1,0:T(8,128)(2,1)} %get-tuple-element.276), channel_id=1, source_target_pairs={{0,8},{8,0},{16,24},{24,16},{1,9},{9,1},{17,25},{25,17},{2,10},{10... | collective-permute-start | bytes 2162696 | tf_op jit(solution)/shard_map/ppermute | solution.py:39
  301.2 19.2 %collective-permute-start.79 = (bf16[22,64,256]{2,1,0:T(8,128)(2,1)S(1)}, bf16[22,64,256]{2,1,0:T(8,128)(2,1)}, u32[]{:S(2)}, u32[]{:S(2)}) collective-permute-start(bf16[22,64,256]{2,1,0:T(8,128)(2,1)S(1)} %pad_maximum_fusion.refs_0_), channel_id=1, source_target_pairs={{0,2},{2,0},{1,3},{3,1},{4,6},{6,4},{5,7},{7,5},{8,10},{10,8},{9,1... | collective-permute-start | bytes 2162696 | tf_op jit(solution)/shard_map/ppermute | solution.py:34
  314.4 17.1 %collective-permute-start.75 = (bf16[8,64,512]{2,1,0:T(8,128)(2,1)}, bf16[8,64,512]{2,1,0:T(8,128)(2,1)S(1)}, u32[]{:S(2)}, u32[]{:S(2)}) collective-permute-start(bf16[8,64,512]{2,1,0:T(8,128)(2,1)} %get-tuple-element.289), channel_id=1, source_target_pairs={{0,2},{2,0},{1,3},{3,1},{4,6},{6,4},{5,7},{7,5},{8,10},{10,8},{9,1... | collective-permute-start | bytes 1572872 | tf_op jit(solution)/shard_map/input_grad/ppermute | solution.py:34
  315.3 16.2 %collective-permute-start.76 = (bf16[8,64,512]{2,1,0:T(8,128)(2,1)}, bf16[8,64,512]{2,1,0:T(8,128)(2,1)S(1)}, u32[]{:S(2)}, u32[]{:S(2)}) collective-permute-start(bf16[8,64,512]{2,1,0:T(8,128)(2,1)} %get-tuple-element.290), channel_id=1, source_target_pairs={{0,4},{4,0},{1,5},{5,1},{2,6},{6,2},{3,7},{7,3},{8,12},{12,8},{9,1... | collective-permute-start | bytes 1572872 | tf_op jit(solution)/shard_map/input_grad/ppermute | solution.py:34
  316.5 24.5 %collective-permute-start.77 = (bf16[8,64,512]{2,1,0:T(8,128)(2,1)}, bf16[8,64,512]{2,1,0:T(8,128)(2,1)S(1)}, u32[]{:S(2)}, u32[]{:S(2)}) collective-permute-start(bf16[8,64,512]{2,1,0:T(8,128)(2,1)} %get-tuple-element.291), channel_id=1, source_target_pairs={{0,6},{2,4},{4,2},{6,0},{1,7},{3,5},{5,3},{7,1},{8,14},{10,12},{12... | collective-permute-start | bytes 1572872 | tf_op jit(solution)/shard_map/input_grad/ppermute | solution.py:43
  320.6 20.4 %collective-permute-start.80 = (bf16[11,64,256]{2,1,0:T(8,128)(2,1)S(1)}, bf16[11,64,256]{2,1,0:T(8,128)(2,1)S(1)}, u32[]{:S(2)}, u32[]{:S(2)}) collective-permute-start(bf16[11,64,256]{2,1,0:T(8,128)(2,1)S(1)} %get-tuple-element.343), channel_id=1, source_target_pairs={{0,24},{8,16},{16,8},{24,0},{1,25},{9,17},{17,9},{25,1},{2,26},{10... | collective-permute-start | bytes 1081352 | tf_op jit(solution)/shard_map/input_grad/ppermute | solution.py:39
  (129 other events, 1188.6 us)

commit v2 on v1

--- a/solution.py
+++ b/solution.py
@@ -782,6 +782,7 @@
         brim = beyond(rim(tiles_out[0], 16), 0, 0)
         deep = rim(tiles_out[2], 32)
         brims = jnp.concatenate([rim(tiles_out[1], 16), deep[:, :16], deep[:, 16:]], axis=2)
+        brims, brim = lax.optimization_barrier((brims, brim))
         brims = beyond(brims, 0, 0)
 
         def both_cores(got):
@@ -891,8 +892,14 @@
             return keep[0]
         return (keep + got.astype(F32)).astype(BF)
 
-    across, pool_part, spread_back, strip_back = lax.optimization_barrier(
-        (across, pool_part, spread_back, strip_back)
+    project_pool = lax.dot_general(
+        joined4.astype(F32),
+        image_heads,
+        (((0,), (0,)), ((), ())),
+        precision=lax.Precision.HIGHEST,
+    ).reshape(feat // half, half, feat)
+    across, pool_part, spread_back, strip_back, project_pool = lax.optimization_barrier(
+        (across, pool_part, spread_back, strip_back, project_pool)
     )
     part3 = weight_grad(0, group3, [(0, 16)])
     arrived2, part3, project_got = lax.optimization_barrier((arrived2, part3, project_got))
@@ -973,12 +980,6 @@
         got, sums1 = lax.optimization_barrier((got, sums1))
         joint, joint_x = gate((joint, joint_x), got)
         pieces32 = [joint, swap(joint, "k"), joint_x, swap(joint_x, "k")]
-        project_pool = lax.dot_general(
-            joined4.astype(F32),
-            image_heads,
-            (((0,), (0,)), ((), ())),
-            precision=lax.Precision.HIGHEST,
-        ).reshape(feat // half, half, feat)
         grad, project_grad = collect(pieces32, 0, [], project_pool)
         project_grad = project_grad.reshape(5 * feat, feat)
         if aligned:

time: 365 us -> 368 us (level)
    ppermute x3, waiting for transfers between devices: 2.81 us -> 11.4 us  [beyond(): return lax.ppermute(x, ('z', 'y', 'x'), pairs)]
    ppermute x46, waiting for transfers between devices: 57 us -> 52.5 us  [swap(): return lax.ppermute(x, axis, SWAP)]
  transfers between devices with their start and end apart: 87 -> 87, of which waited for: 47 -> 45; matrix products, arithmetic and copies ran while one was open for 6% -> 5% of each run, Pallas kernels for 25% -> 25%
where the time goes in v2:
time: 368 us; the launch traced here: 366 us
  Pallas kernels  113 us (31%)
  waiting for transfers between devices  105 us (29%)
  starting transfers between devices  84.7 us (23%)
  other arithmetic  19 us (5%)
  matrix products  14.2 us (4%)
  local copies, waits for them, and re-layouts  13.4 us (4%)
  blocking collectives  13.1 us (4%)
  between operations  4.21 us (1%)
    pallas_call x12, Pallas kernels, call(): pl.pallas_call(kernel, name=name, in_specs=in_specs, out_specs=out_specs...  113 us
    ppermute x46, waiting for transfers between devices, swap(): return lax.ppermute(x, axis, SWAP)  52.5 us
    ppermute x46, starting transfers between devices, swap(): return lax.ppermute(x, axis, SWAP)  34.5 us
    ppermute x24, starting transfers between devices, quad(): lax.ppermute(x, axes, [(i, i ^ step) for i in range(4)])  29.3 us
    ppermute x24, waiting for transfers between devices, quad(): lax.ppermute(x, axes, [(i, i ^ step) for i in range(4)])  24.2 us
    all_to_all x1, blocking collectives, per_device(): halo = lax.all_to_all(halo, ('y', 'x'), 0, 0)  13.1 us
    ppermute x3, waiting for transfers between devices, beyond(): return lax.ppermute(x, ('z', 'y', 'x'), pairs)  11.4 us
    ppermute x5, waiting for transfers between devices, crossed(): return lax.ppermute(x, ('y', 'x'), [(i, 3 - i) for i in range(4)])  11 us
  transfers between devices with their start and end apart: 87, of which 45 were waited for; matrix products, arithmetic and copies ran while one was open for 5% of the time, Pallas kernels for 25%

profile of v2, /device:TPU:0, one launch (start us, length us, event | category | flops | bytes accessed | tf_op | source)
XLA Modules:
  0.0 366.1 jit_solution(16060976986952018138)
XLA Ops:
  4.8 4.3 %pack.1 = (bf16[8,64,512]{2,1,0:T(8,128)(2,1)}, bf16[8,64,512]{2,1,0:T(8,128)(2,1)}, bf16[8,64,512]{2,1,0:T(8,128)(2,1)}, bf16[8,64,512]{2,1,0:T(8,128)(2,1)}, bf16[4,8,24,512]{3,2,1,0:T(8,128)(2,1)}) custom-call(s32[5]{0:T(128)} %stack.127.info, bf16[64,8,2048]{2,1,0:T(8,128)(2,1)} %full.1, bf16[1,512]{1,0:T(2,128)(2,1)} %broadcast_in_dim.38.marks), custom_call_target="tpu_custom_call" | custom-call | bytes 10000000 | tf_op jit(solution)/shard_map/spread_features/pack/pallas_call | solution.py:482
  13.5 3.8 %collective-permute-start.2 = (bf16[8,64,512]{2,1,0:T(8,128)(2,1)}, bf16[8,64,512]{2,1,0:T(8,128)(2,1)}, u32[]{:S(2)}, u32[]{:S(2)}) collective-permute-start(bf16[8,64,512]{2,1,0:T(8,128)(2,1)} %get-tuple-element.168), channel_id=1, source_target_pairs={{0,4},{4,0},{1,5},{5,1},{2,6},{6,2},{3,7},{7,3},{8,12},{12,8},{9,1... | collective-permute-start | bytes 1572872 | tf_op jit(solution)/shard_map/spread_features/ppermute | solution.py:34
  17.4 9.2 %collective-permute-done.1.refs_1_ = bf16[8,64,512]{2,1,0:T(8,128)(2,1)} collective-permute-done((bf16[8,64,512]{2,1,0:T(8,128)(2,1)}, bf16[8,64,512]{2,1,0:T(8,128)(2,1)}, u32[]{:S(2)}, u32[]{:S(2)}) %collective-permute-start.1) | collective-permute-done | bytes 524320 | tf_op jit(solution)/shard_map/spread_features/ppermute | solution.py:34
  26.6 13.0 %collective-permute-done.2.refs_2_ = bf16[8,64,512]{2,1,0:T(8,128)(2,1)} collective-permute-done((bf16[8,64,512]{2,1,0:T(8,128)(2,1)}, bf16[8,64,512]{2,1,0:T(8,128)(2,1)}, u32[]{:S(2)}, u32[]{:S(2)}) %collective-permute-start.2) | collective-permute-done | bytes 524320 | tf_op jit(solution)/shard_map/spread_features/ppermute | solution.py:34
  40.9 13.1 %all_to_all.10.refs_8_ = bf16[4,8,24,512]{3,2,1,0:T(8,128)(2,1)S(1)} all-to-all(bf16[4,8,24,512]{3,2,1,0:T(8,128)(2,1)S(1)} %dynamic_update_slice.3), channel_id=1, replica_groups=mesh['z'=4,'y'=2,'x'=2,'k'=2] {'y','x'}, dimensions={0} | all-to-all | bytes 1572864 | tf_op jit(solution)/shard_map/spread_features/all_to_all | solution.py:573
  60.5 11.7 %forward_taps.2 = (f32[2,8,64,256]{3,2,1,0:T(8,128)}, bf16[2,8,64,256]{3,2,1,0:T(8,128)(2,1)}, f32[2,8,64,256]{3,2,1,0:T(8,128)}, bf16[2,8,64,256]{3,2,1,0:T(8,128)(2,1)}) custom-call(s32[5]{0:T(128)} %stack.132.info, bf16[8,64,512]{2,1,0:T(8,128)(2,1)} %get-tuple-element.193.refs_0_, bf16[8,64,512]{2,1,0:T(8,128)(2,1)} %collective-permute-done.1.refs_1_, ...), custom_call_target="tpu_custom_call" | custom-call | flops 8053063680 | bytes 10000000 | tf_op jit(solution)/shard_map/forward_taps/pallas_call | solution.py:482
  73.7 16.5 %forward_taps.3 = (f32[2,8,64,256]{3,2,1,0:T(8,128)}, bf16[2,8,64,256]{3,2,1,0:T(8,128)(2,1)}, f32[2,8,64,256]{3,2,1,0:T(8,128)}, bf16[2,8,64,256]{3,2,1,0:T(8,128)(2,1)}) custom-call(s32[5]{0:T(128)} %stack.132.info, bf16[8,64,512]{2,1,0:T(8,128)(2,1)} %get-tuple-element.193.refs_0_, bf16[8,64,512]{2,1,0:T(8,128)(2,1)} %collective-permute-done.1.refs_1_, ...), custom_call_target="tpu_custom_call" | custom-call | flops 8053063680 | bytes 10000000 | tf_op jit(solution)/shard_map/forward_taps/pallas_call | solution.py:482
  94.8 4.9 %collective-permute-done.12 = bf16[8,64,256]{2,1,0:T(8,128)(2,1)S(1)} collective-permute-done((bf16[8,64,256]{2,1,0:T(8,128)(2,1)S(1)}, bf16[8,64,256]{2,1,0:T(8,128)(2,1)S(1)}, u32[]{:S(2)}, u32[]{:S(2)}) %collective-permute-start.12) | collective-permute-done | bytes 262176 | tf_op jit(solution)/shard_map/ppermute | solution.py:34
  101.2 5.8 %across.1 = (bf16[256,4096]{1,0:T(8,128)(2,1)}, f32[128,512]{1,0:T(8,128)}, f32[1,512]{1,0:T(1,128)}) custom-call(s32[5]{0:T(128)} %stack.132.info, bf16[8,64,512]{2,1,0:T(8,128)(2,1)} %get-tuple-element.193.refs_0_, bf16[8,64,512]{2,1,0:T(8,128)(2,1)} %collective-permute-done.1.refs_1_, bf16[8,64,512]{2,1,0:T(8,128)(2,1)} %collective-permute-done.2.refs_2_, ...), custom_call_target="tpu_custom_call" | custom-call | flops 2000000000 | bytes 10000000 | tf_op jit(solution)/shard_map/across/across/pallas_call | solution.py:482
  172.3 3.4 fusion.86
  195.7 4.8 %collective-permute-done.45 = bf16[8,16,256]{2,1,0:T(8,128)(2,1)S(1)} collective-permute-done((bf16[8,16,256]{2,1,0:T(8,128)(2,1)S(1)}, bf16[8,16,256]{2,1,0:T(8,128)(2,1)S(1)}, u32[]{:S(2)}, u32[]{:S(2)}) %collective-permute-start.45) | collective-permute-done | bytes 65568 | tf_op jit(solution)/shard_map/spread_slopes/ppermute | solution.py:533
  209.9 3.5 all-to-all-start.1
  215.9 6.6 %collective-permute-done.49 = bf16[8,16,768]{2,1,0:T(8,128)(2,1)S(1)} collective-permute-done((bf16[8,16,768]{2,1,0:T(8,128)(2,1)S(1)}, bf16[8,16,768]{2,1,0:T(8,128)(2,1)S(1)}, u32[]{:S(2)}, u32[]{:S(2)}) %collective-permute-start.49) | collective-permute-done | bytes 196640 | tf_op jit(solution)/shard_map/spread_slopes/ppermute | solution.py:533
  229.6 11.5 %weight_taps.3 = (bf16[2,9,64,256]{3,2,1,0:T(8,128)(2,1)}, bf16[2,9,64,256]{3,2,1,0:T(8,128)(2,1)}) custom-call(s32[5]{0:T(128)} %stack.132.info, bf16[8,80,256]{2,1,0:T(8,128)(2,1)} %copy-done.22, bf16[8,80,256]{2,1,0:T(8,128)(2,1)} %collective-permute-done.46.refs_1_, bf16[8,80,256]{2,1,0:T(8,128)(2,1)} %collective-permute-done.47.refs_2_, ...), custom_call_target="tpu_custom_call" | custom-call | flops 8053063680 | bytes 10000000 | tf_op jit(solution)/shard_map/weight_taps/pallas_call | solution.py:482
  251.0 10.2 %weight_taps.4 = (bf16[2,9,64,256]{3,2,1,0:T(8,128)(2,1)}, bf16[2,9,64,256]{3,2,1,0:T(8,128)(2,1)}) custom-call(s32[5]{0:T(128)} %stack.132.info, bf16[8,80,256]{2,1,0:T(8,128)(2,1)} %copy-done.23, bf16[8,80,256]{2,1,0:T(8,128)(2,1)} %collective-permute-done.54.refs_1_.refs_9_, bf16[8,80,256]{2,1,0:T(8,128)(2,1)} %copy-done.68, ...), custom_call_target="tpu_custom_call" | custom-call | flops 8053063680 | bytes 10000000 | tf_op jit(solution)/shard_map/weight_taps/pallas_call | solution.py:482
  266.4 16.1 %input_taps.2.refs_11_ = f32[2,8,128,512]{3,2,1,0:T(8,128)} custom-call(s32[5]{0:T(128)} %stack.132.info, bf16[8,80,256]{2,1,0:T(8,128)(2,1)} %copy-done.22, bf16[8,80,256]{2,1,0:T(8,128)(2,1)} %collective-permute-done.46.refs_1_, bf16[8,80,256]{2,1,0:T(8,128)(2,1)} %collective-permute-done.47.refs_2_, bf16[8,80,256]{2,1,0:T(8,128)(2,1)} %copy-done.64, ...), custom_call_target="tpu_custom_call" | custom-call | flops 10737418240 | bytes 10000000 | tf_op jit(solution)/shard_map/input_grad/input_taps/pallas_call | solution.py:482
  282.5 3.1 collective-permute-done.68
  292.9 11.1 %weight_taps.5 = (bf16[2,11,64,256]{3,2,1,0:T(8,128)(2,1)}, bf16[2,11,64,256]{3,2,1,0:T(8,128)(2,1)}) custom-call(s32[5]{0:T(128)} %stack.132.info, bf16[8,160,256]{2,1,0:T(8,128)(2,1)} %copy-done.16, bf16[8,160,256]{2,1,0:T(8,128)(2,1)} %collective-permute-done.62.refs_1_, bf16[8,160,256]{2,1,0:T(8,128)(2,1)} %collective-permute-done.63.refs_2_, ...), custom_call_target="tpu_custom_call" | custom-call | flops 8053063680 | bytes 10000000 | tf_op jit(solution)/shard_map/weight_taps/pallas_call | solution.py:482
  306.1 12.6 %input_taps.3 = (bf16[8,64,512]{2,1,0:T(8,128)(2,1)}, bf16[8,64,512]{2,1,0:T(8,128)(2,1)}, bf16[8,64,512]{2,1,0:T(8,128)(2,1)}, bf16[8,64,512]{2,1,0:T(8,128)(2,1)}) custom-call(s32[5]{0:T(128)} %stack.132.info, bf16[8,160,256]{2,1,0:T(8,128)(2,1)} %copy-done.16, bf16[8,160,256]{2,1,0:T(8,128)(2,1)} %collective-permute-done.62.refs_1_, ...), custom_call_target="tpu_custom_call" | custom-call | flops 10737418240 | bytes 10000000 | tf_op jit(solution)/shard_map/input_grad/input_taps/pallas_call | solution.py:482
  326.0 8.8 %collective-permute-done.75.refs_1_ = bf16[8,64,512]{2,1,0:T(8,128)(2,1)S(1)} collective-permute-done((bf16[8,64,512]{2,1,0:T(8,128)(2,1)}, bf16[8,64,512]{2,1,0:T(8,128)(2,1)S(1)}, u32[]{:S(2)}, u32[]{:S(2)}) %collective-permute-start.75) | collective-permute-done | bytes 524320 | tf_op jit(solution)/shard_map/input_grad/ppermute | solution.py:34
  334.8 10.2 %collective-permute-done.77.refs_3_ = bf16[8,64,512]{2,1,0:T(8,128)(2,1)S(1)} collective-permute-done((bf16[8,64,512]{2,1,0:T(8,128)(2,1)}, bf16[8,64,512]{2,1,0:T(8,128)(2,1)S(1)}, u32[]{:S(2)}, u32[]{:S(2)}) %collective-permute-start.77) | collective-permute-done | bytes 524320 | tf_op jit(solution)/shard_map/input_grad/ppermute | solution.py:43
  347.4 3.6 unpack.1
  352.8 5.4 %collect.2 = (f32[27,4,64,256]{3,2,1,0:T(8,128)}, f32[5,4,64,256]{3,2,1,0:T(8,128)}) custom-call(s32[5]{0:T(128)} %stack.127.info, bf16[22,64,256]{2,1,0:T(8,128)(2,1)} %copy-done.14, bf16[22,64,256]{2,1,0:T(8,128)(2,1)} %copy-done.55, bf16[22,64,256]{2,1,0:T(8,128)(2,1)} %copy-done.54, bf16[22,64,256]{2,1,0:T(8,128)(2,1)} %copy-done.56, f32[4,64,256]{2,1,0:T(8,128)} %bitcast.183), custom_call_target="tpu_custom_call" | custom-call | flops 6000000000 | bytes 10000000 | tf_op jit(solution)/shard_map/input_grad/collect/pallas_call | solution.py:482
  362.1 3.8 %collect.3 = (f32[27,4,64,256]{3,2,1,0:T(8,128)}, f32[4,1,64,256]{3,2,1,0:T(8,128)}, f32[4,1,64,256]{3,2,1,0:T(8,128)}) custom-call(s32[5]{0:T(128)} %stack.127.info, bf16[11,64,256]{2,1,0:T(8,128)(2,1)} %copy-done.21, bf16[11,64,256]{2,1,0:T(8,128)(2,1)} %collective-permute-done.84.refs_1_, ...), custom_call_target="tpu_custom_call", output_to_operand_aliasing={{0}: (5, {})} | custom-call | flops 6000000000 | bytes 10000000 | tf_op jit(solution)/shard_map/collect/pallas_call | solution.py:482
  (429 shorter events, 164.9 us)
Async XLA Ops:
  9.1 31.2 %collective-permute-start = (bf16[4,8,24,512]{3,2,1,0:T(8,128)(2,1)}, bf16[4,8,24,512]{3,2,1,0:T(8,128)(2,1)S(1)}, u32[]{:S(2)}, u32[]{:S(2)}) collective-permute-start(bf16[4,8,24,512]{3,2,1,0:T(8,128)(2,1)} %get-tuple-element.165), channel_id=1, source_target_pairs={{4,12},{6,14},{8,0},{10,2},{12,20},{14,22},{16,8},{18,10},{20,28},... | collective-permute-start | bytes 2359304 | tf_op jit(solution)/shard_map/spread_features/ppermute | solution.py:533
  10.5 16.1 %collective-permute-start.1 = (bf16[8,64,512]{2,1,0:T(8,128)(2,1)}, bf16[8,64,512]{2,1,0:T(8,128)(2,1)}, u32[]{:S(2)}, u32[]{:S(2)}) collective-permute-start(bf16[8,64,512]{2,1,0:T(8,128)(2,1)} %get-tuple-element.167), channel_id=1, source_target_pairs={{0,2},{2,0},{1,3},{3,1},{4,6},{6,4},{5,7},{7,5},{8,10},{10,8},{9,1... | collective-permute-start | bytes 1572872 | tf_op jit(solution)/shard_map/spread_features/ppermute | solution.py:34
  13.5 26.0 %collective-permute-start.2 = (bf16[8,64,512]{2,1,0:T(8,128)(2,1)}, bf16[8,64,512]{2,1,0:T(8,128)(2,1)}, u32[]{:S(2)}, u32[]{:S(2)}) collective-permute-start(bf16[8,64,512]{2,1,0:T(8,128)(2,1)} %get-tuple-element.168), channel_id=1, source_target_pairs={{0,4},{4,0},{1,5},{5,1},{2,6},{6,2},{3,7},{7,3},{8,12},{12,8},{9,1... | collective-permute-start | bytes 1572872 | tf_op jit(solution)/shard_map/spread_features/ppermute | solution.py:34
  17.4 22.9 %collective-permute-start.3 = (bf16[8,64,512]{2,1,0:T(8,128)(2,1)}, bf16[8,64,512]{2,1,0:T(8,128)(2,1)}, u32[]{:S(2)}, u32[]{:S(2)}) collective-permute-start(bf16[8,64,512]{2,1,0:T(8,128)(2,1)} %get-tuple-element.169), channel_id=1, source_target_pairs={{0,6},{2,4},{4,2},{6,0},{1,7},{3,5},{5,3},{7,1},{8,14},{10,12},{12... | collective-permute-start | bytes 1572872 | tf_op jit(solution)/shard_map/spread_features/ppermute | solution.py:43
  72.2 18.1 %collective-permute-start.9 = (bf16[2,8,64,256]{3,2,1,0:T(8,128)(2,1)}, bf16[2,8,64,256]{3,2,1,0:T(8,128)(2,1)S(1)}, u32[]{:S(2)}, u32[]{:S(2)}) collective-permute-start(bf16[2,8,64,256]{3,2,1,0:T(8,128)(2,1)} %get-tuple-element.176), channel_id=1, source_target_pairs={{0,2},{2,0},{1,3},{3,1},{4,6},{6,4},{5,7},{7,5},{8,10},{10,8},{9,1... | collective-permute-start | bytes 1572872 | tf_op jit(solution)/shard_map/ppermute | solution.py:34
  73.2 17.1 %collective-permute-start.10 = (bf16[2,8,64,256]{3,2,1,0:T(8,128)(2,1)}, bf16[2,8,64,256]{3,2,1,0:T(8,128)(2,1)S(1)}, u32[]{:S(2)}, u32[]{:S(2)}) collective-permute-start(bf16[2,8,64,256]{3,2,1,0:T(8,128)(2,1)} %get-tuple-element.178), channel_id=1, source_target_pairs={{0,4},{4,0},{1,5},{5,1},{2,6},{6,2},{3,7},{7,3},{8,12},{12,8},{9,1... | collective-permute-start | bytes 1572872 | tf_op jit(solution)/shard_map/ppermute | solution.py:34
  93.2 16.6 %collective-permute-start.13 = (bf16[2,8,64,256]{3,2,1,0:T(8,128)(2,1)}, bf16[2,8,64,256]{3,2,1,0:T(8,128)(2,1)}, u32[]{:S(2)}, u32[]{:S(2)}) collective-permute-start(bf16[2,8,64,256]{3,2,1,0:T(8,128)(2,1)} %get-tuple-element.190), channel_id=1, source_target_pairs={{0,2},{2,0},{1,3},{3,1},{4,6},{6,4},{5,7},{7,5},{8,10},{10,8},{9,1... | collective-permute-start | bytes 1572872 | tf_op jit(solution)/shard_map/ppermute | solution.py:34
  200.5 22.1 %collective-permute-start.48 = (bf16[8,80,256]{2,1,0:T(8,128)(2,1)S(1)}, bf16[8,80,256]{2,1,0:T(8,128)(2,1)S(1)}, u32[]{:S(2)}, u32[]{:S(2)}) collective-permute-start(bf16[8,80,256]{2,1,0:T(8,128)(2,1)S(1)} %pad_maximum_fusion.2.refs_0_), channel_id=1, source_target_pairs={{0,6},{2,4},{4,2},{6,0},{1,7},{3,5},{5,3},{7,1},{8,14},{10,12},{12... | collective-permute-start | bytes 983048 | tf_op jit(solution)/shard_map/spread_slopes/ppermute | solution.py:43
  200.6 22.0 %collective-permute-start.47 = (bf16[8,80,256]{2,1,0:T(8,128)(2,1)S(1)}, bf16[8,80,256]{2,1,0:T(8,128)(2,1)}, u32[]{:S(2)}, u32[]{:S(2)}) collective-permute-start(bf16[8,80,256]{2,1,0:T(8,128)(2,1)S(1)} %pad_maximum_fusion.2.refs_0_), channel_id=1, source_target_pairs={{0,4},{4,0},{1,5},{5,1},{2,6},{6,2},{3,7},{7,3},{8,12},{12,8},{9,1... | collective-permute-start | bytes 983048 | tf_op jit(solution)/shard_map/spread_slopes/ppermute | solution.py:34
  203.4 19.2 %collective-permute-start.46 = (bf16[8,80,256]{2,1,0:T(8,128)(2,1)S(1)}, bf16[8,80,256]{2,1,0:T(8,128)(2,1)}, u32[]{:S(2)}, u32[]{:S(2)}) collective-permute-start(bf16[8,80,256]{2,1,0:T(8,128)(2,1)S(1)} %pad_maximum_fusion.2.refs_0_), channel_id=1, source_target_pairs={{0,2},{2,0},{1,3},{3,1},{4,6},{6,4},{5,7},{7,5},{8,10},{10,8},{9,1... | collective-permute-start | bytes 983048 | tf_op jit(solution)/shard_map/spread_slopes/ppermute | solution.py:34
  223.9 17.2 %collective-permute-start.57 = (bf16[256,256]{1,0:T(8,128)(2,1)S(1)}, bf16[256,256]{1,0:T(8,128)(2,1)S(1)}, u32[]{:S(2)}, u32[]{:S(2)}) collective-permute-start(bf16[256,256]{1,0:T(8,128)(2,1)S(1)} %reduce_sum.224), channel_id=1, source_target_pairs={{0,8},{8,0},{16,24},{24,16},{1,9},{9,1},{17,25},{25,17},{2,10},{10... | collective-permute-start | bytes 393224 | tf_op jit(solution)/shard_map/spread_slopes/ppermute | solution.py:39
  226.5 17.2 %collective-permute-start.55 = (bf16[8,80,256]{2,1,0:T(8,128)(2,1)S(1)}, bf16[8,80,256]{2,1,0:T(8,128)(2,1)S(1)}, u32[]{:S(2)}, u32[]{:S(2)}) collective-permute-start(bf16[8,80,256]{2,1,0:T(8,128)(2,1)S(1)} %pad_maximum_fusion.3.refs_0_.refs_8_), channel_id=1, source_target_pairs={{0,4},{4,0},{1,5},{5,1},{2,6},{6,2},{3,7},{7,3},{8,12},{12,8},{9,1... | collective-permute-start | bytes 983048 | tf_op jit(solution)/shard_map/spread_slopes/ppermute | solution.py:34
  244.9 16.3 %collective-permute-start.65 = (bf16[256,256]{1,0:T(8,128)(2,1)S(1)}, bf16[256,256]{1,0:T(8,128)(2,1)S(1)}, u32[]{:S(2)}, u32[]{:S(2)}) collective-permute-start(bf16[256,256]{1,0:T(8,128)(2,1)S(1)} %add_convert_fusion.12), channel_id=1, source_target_pairs={{0,16},{8,24},{16,0},{24,8},{1,17},{9,25},{17,1},{25,9},{2,18},{10... | collective-permute-start | bytes 393224 | tf_op jit(solution)/shard_map/ppermute | solution.py:39
  245.6 18.4 %collective-permute-start.66 = (bf16[2,9,64,256]{3,2,1,0:T(8,128)(2,1)}, bf16[2,9,64,256]{3,2,1,0:T(8,128)(2,1)S(1)}, u32[]{:S(2)}, u32[]{:S(2)}) collective-permute-start(bf16[2,9,64,256]{3,2,1,0:T(8,128)(2,1)} %get-tuple-element.253), channel_id=1, source_target_pairs={{0,8},{8,0},{16,24},{24,16},{1,9},{9,1},{17,25},{25,17},{2,10},{10... | collective-permute-start | bytes 1769480 | tf_op jit(solution)/shard_map/ppermute | solution.py:39
  247.4 38.2 %collective-permute-start.64 = (bf16[8,160,256]{2,1,0:T(8,128)(2,1)S(1)}, bf16[8,160,256]{2,1,0:T(8,128)(2,1)}, u32[]{:S(2)}, u32[]{:S(2)}) collective-permute-start(bf16[8,160,256]{2,1,0:T(8,128)(2,1)S(1)} %pad_maximum_fusion.1.refs_0_), channel_id=1, source_target_pairs={{0,6},{2,4},{4,2},{6,0},{1,7},{3,5},{5,3},{7,1},{8,14},{10,12},{12... | collective-permute-start | bytes 1966088 | tf_op jit(solution)/shard_map/ppermute | solution.py:43
  249.1 36.6 %collective-permute-start.63 = (bf16[8,160,256]{2,1,0:T(8,128)(2,1)S(1)}, bf16[8,160,256]{2,1,0:T(8,128)(2,1)}, u32[]{:S(2)}, u32[]{:S(2)}) collective-permute-start(bf16[8,160,256]{2,1,0:T(8,128)(2,1)S(1)} %pad_maximum_fusion.1.refs_0_), channel_id=1, source_target_pairs={{0,4},{4,0},{1,5},{5,1},{2,6},{6,2},{3,7},{7,3},{8,12},{12,8},{9,1... | collective-permute-start | bytes 1966088 | tf_op jit(solution)/shard_map/ppermute | solution.py:34
  250.7 35.0 %collective-permute-start.62 = (bf16[8,160,256]{2,1,0:T(8,128)(2,1)S(1)}, bf16[8,160,256]{2,1,0:T(8,128)(2,1)}, u32[]{:S(2)}, u32[]{:S(2)}) collective-permute-start(bf16[8,160,256]{2,1,0:T(8,128)(2,1)S(1)} %pad_maximum_fusion.1.refs_0_), channel_id=1, source_target_pairs={{0,2},{2,0},{1,3},{3,1},{4,6},{6,4},{5,7},{7,5},{8,10},{10,8},{9,1... | collective-permute-start | bytes 1966088 | tf_op jit(solution)/shard_map/ppermute | solution.py:34
  264.0 21.7 %collective-permute-start.67 = (bf16[2,9,64,256]{3,2,1,0:T(8,128)(2,1)}, bf16[2,9,64,256]{3,2,1,0:T(8,128)(2,1)S(1)}, u32[]{:S(2)}, u32[]{:S(2)}) collective-permute-start(bf16[2,9,64,256]{3,2,1,0:T(8,128)(2,1)} %get-tuple-element.263), channel_id=1, source_target_pairs={{0,8},{8,0},{16,24},{24,16},{1,9},{9,1},{17,25},{25,17},{2,10},{10... | collective-permute-start | bytes 1769480 | tf_op jit(solution)/shard_map/ppermute | solution.py:39
  264.1 21.5 %collective-permute-start.68 = (bf16[9,64,256]{2,1,0:T(8,128)(2,1)S(1)}, bf16[9,64,256]{2,1,0:T(8,128)(2,1)S(1)}, u32[]{:S(2)}, u32[]{:S(2)}) collective-permute-start(bf16[9,64,256]{2,1,0:T(8,128)(2,1)S(1)} %get-tuple-element.353), channel_id=1, source_target_pairs={{0,24},{8,16},{16,8},{24,0},{1,25},{9,17},{17,9},{25,1},{2,26},{10... | collective-permute-start | bytes 884744 | tf_op jit(solution)/shard_map/ppermute | solution.py:39
  304.1 19.5 %collective-permute-start.78 = (bf16[2,11,64,256]{3,2,1,0:T(8,128)(2,1)}, bf16[2,11,64,256]{3,2,1,0:T(8,128)(2,1)S(1)}, u32[]{:S(2)}, u32[]{:S(2)}) collective-permute-start(bf16[2,11,64,256]{3,2,1,0:T(8,128)(2,1)} %get-tuple-element.281), channel_id=1, source_target_pairs={{0,8},{8,0},{16,24},{24,16},{1,9},{9,1},{17,25},{25,17},{2,10},{10... | collective-permute-start | bytes 2162696 | tf_op jit(solution)/shard_map/ppermute | solution.py:39
  304.4 19.1 %collective-permute-start.79 = (bf16[22,64,256]{2,1,0:T(8,128)(2,1)S(1)}, bf16[22,64,256]{2,1,0:T(8,128)(2,1)S(1)}, u32[]{:S(2)}, u32[]{:S(2)}) collective-permute-start(bf16[22,64,256]{2,1,0:T(8,128)(2,1)S(1)} %pad_maximum_fusion.refs_0_), channel_id=1, source_target_pairs={{0,2},{2,0},{1,3},{3,1},{4,6},{6,4},{5,7},{7,5},{8,10},{10,8},{9,1... | collective-permute-start | bytes 2162696 | tf_op jit(solution)/shard_map/ppermute | solution.py:34
  318.8 16.0 %collective-permute-start.75 = (bf16[8,64,512]{2,1,0:T(8,128)(2,1)}, bf16[8,64,512]{2,1,0:T(8,128)(2,1)S(1)}, u32[]{:S(2)}, u32[]{:S(2)}) collective-permute-start(bf16[8,64,512]{2,1,0:T(8,128)(2,1)} %get-tuple-element.294), channel_id=1, source_target_pairs={{0,2},{2,0},{1,3},{3,1},{4,6},{6,4},{5,7},{7,5},{8,10},{10,8},{9,1... | collective-permute-start | bytes 1572872 | tf_op jit(solution)/shard_map/input_grad/ppermute | solution.py:34
  320.3 24.7 %collective-permute-start.77 = (bf16[8,64,512]{2,1,0:T(8,128)(2,1)}, bf16[8,64,512]{2,1,0:T(8,128)(2,1)S(1)}, u32[]{:S(2)}, u32[]{:S(2)}) collective-permute-start(bf16[8,64,512]{2,1,0:T(8,128)(2,1)} %get-tuple-element.296), channel_id=1, source_target_pairs={{0,6},{2,4},{4,2},{6,0},{1,7},{3,5},{5,3},{7,1},{8,14},{10,12},{12... | collective-permute-start | bytes 1572872 | tf_op jit(solution)/shard_map/input_grad/ppermute | solution.py:43
  323.8 21.2 %collective-permute-start.80 = (bf16[11,64,256]{2,1,0:T(8,128)(2,1)S(1)}, bf16[11,64,256]{2,1,0:T(8,128)(2,1)S(1)}, u32[]{:S(2)}, u32[]{:S(2)}) collective-permute-start(bf16[11,64,256]{2,1,0:T(8,128)(2,1)S(1)} %get-tuple-element.349), channel_id=1, source_target_pairs={{0,24},{8,16},{16,8},{24,0},{1,25},{9,17},{17,9},{25,1},{2,26},{10... | collective-permute-start | bytes 1081352 | tf_op jit(solution)/shard_map/input_grad/ppermute | solution.py:39
  (135 other events, 1252.7 us)
